TPU v7x, 32 devices: a whole 2x2x4 slice. The times are simulated.
32 devices in a mesh: chan: 16 (over z, y, core), seg: 2 (over x).
Axes of the slice: x: 2, y: 2, z: 4, core: 2. Of those that a mesh axis runs over, the one named last changes fastest.
Arguments:
- signal: bfloat16 [16, 1024, 4096], P('seg', None, 'chan'), may hold values from -150 to 150
- band: int32 [16, 4], replicated, may hold values from 0 to 192
- sched: int32 [16, 4], P('chan'), may hold values 0 or 1
Outputs:
- cross: bfloat16 [16, 4, 2, 64, 256, 256], P('chan', None, None, 'seg')
All inputs are finite; a program needn't handle non-finite values. No bound on the sum of `sched` on one device may be relied on, other than what follows from the above.
Results may differ from a plain program's by a relative error of at most 0.0067.
Values may be sent and summed in bfloat16 or wider, within the bound.
No kernel may reach another device: no remote copies, remote signals or barrier semaphores. Data moves between devices by JAX's collectives and lax.ppermute only.
A program may use at most 192 MiB of HBM per device.

v0:
```python
import math

import jax
import jax.numpy as jnp
from jax import lax
from jax.sharding import PartitionSpec as P

NB = 256
BW = 64
PAIRS = 4


def from_behind(block, axis, distance):
    devices = range(lax.axis_size(axis))
    route = [((i - distance) % len(devices), i) for i in devices]
    return lax.ppermute(block, axis, route)


def dft_table(nbins, length):
    freq = jnp.arange(nbins, dtype=jnp.int32)[:, None]
    sample = jnp.arange(length, dtype=jnp.int32)[None, :]
    phase = (freq * sample % length).astype(jnp.float32) * (2.0 * math.pi / length)
    window = 0.5 - 0.5 * jnp.cos(sample.astype(jnp.float32) * (2.0 * math.pi / length))
    return jnp.stack([window * jnp.cos(phase), -window * jnp.sin(phase)]).astype(jnp.bfloat16)


def pair_cross(first, second):
    stacked = jnp.concatenate([first[:, 0], first[:, 1]], axis=0)
    real_side = jnp.concatenate([second[:, 0], second[:, 1]], axis=0)
    imag_side = jnp.concatenate([-second[:, 1], second[:, 0]], axis=0)
    partner = jnp.stack([real_side, imag_side])
    return jnp.einsum("sfi,rsfj->rfij", stacked, partner, preferred_element_type=jnp.float32)


def body(signal, band, sched):
    seg_dev, length, width = signal.shape
    segs = seg_dev * lax.axis_size("seg")
    power = lax.psum(jnp.sum(jnp.square(signal.astype(jnp.float32)), axis=(0, 1)), "seg")
    inv_rms = lax.rsqrt(power / (segs * length) + 1e-06)
    table = dft_table(NB, length)
    raw = jnp.einsum("rfl,slc->srfc", table, signal, preferred_element_type=jnp.float32)
    spectra = (raw * inv_rms).astype(jnp.bfloat16)
    block = lax.axis_index("chan")
    scale = 1.0 / (segs * 0.375 * length)
    results = []
    for pair in range(PAIRS):
        offset = band[block, pair]
        own = lax.dynamic_slice_in_dim(spectra, offset, BW, 2)
        if pair == 0:
            arrived = (lax.all_to_all(own, "seg", split_axis=2, concat_axis=0, tiled=True),)
            mine = arrived[0]
            theirs = mine
        else:
            moved = from_behind(spectra, "chan", -pair)
            other = lax.dynamic_slice_in_dim(moved, offset, BW, 2)
            mine, theirs = (
                lax.all_to_all(own, "seg", split_axis=2, concat_axis=0, tiled=True),
                lax.all_to_all(other, "seg", split_axis=2, concat_axis=0, tiled=True),
            )
        live = sched[0, pair]
        result = pair_cross(mine, theirs) * scale * live.astype(jnp.float32)
        results.append(result.astype(jnp.bfloat16))
    return jnp.stack(results)[None]


def solution(mesh):
    in_specs = (P("seg", None, "chan"), P(), P("chan", None))
    out_specs = P("chan", None, None, "seg", None, None)
    return jax.shard_map(body, mesh=mesh, in_specs=in_specs, out_specs=out_specs, check_vma=False)
```

profile of v0, /device:TPU:0, one launch (start us, length us, event | category | flops | bytes accessed | tf_op | source)
XLA Modules:
  0.0 264.9 jit_solution(11574314686353061704)
XLA Ops:
  0.0 1.5 constant_dynamic-slice_fusion.3
  6.8 3.3 %multiply_reduce_fusion = f32[256]{0:T(256)S(1)} fusion(bf16[8,1024,256]{2,1,0:T(8,128)(2,1)} %param.3), kind=kLoop, calls=%fused_computation.5 | loop fusion | flops 6291200 | bytes 4195328 | tf_op jit(solution)/shard_map/reduce_sum | solution.py:38
  10.1 5.8 %psum.7 = f32[256]{0:T(256)S(1)} all-reduce(f32[256]{0:T(256)S(1)} %multiply_reduce_fusion), channel_id=1, replica_groups=mesh['chan'=16,'seg'=2] {'seg'}, use_global_device_ids=true, to_apply=%region_1.0 | all-reduce | flops 256 | bytes 2048 | tf_op jit(solution)/shard_map/psum | solution.py:38
  18.5 4.5 %multiply_convert_fusion.5 = (bf16[1,256,1024]{2,1,0:T(8,128)(2,1)S(1)}, bf16[1,256,1024]{2,1,0:T(8,128)(2,1)S(1)}) fusion(f32[1024]{0:T(1024)S(1)} %fusion.34, f32[1024]{0:T(1024)S(1)} %multiply_subtract_fusion), kind=kLoop, calls=%fused_computation.33 | loop fusion | flops 4718592 | bytes 1056768 | tf_op jit(solution)/shard_map/convert.1
  23.0 4.5 %multiply_convert_fusion.4 = bf16[2,256,8,256]{3,1,2,0:T(8,128)(2,1)S(1)} fusion(bf16[8,1024,256]{2,1,0:T(8,128)(2,1)} %param.3, f32[256]{0:T(256)S(1)} %add_rsqrt_fusion, bf16[1,256,1024]{2,1,0:T(8,128)(2,1)S(1)} %get-tuple-element.39, bf16[1,256,1024]{2,1,0:T(8,128)(2,1)S(1)} %get-tuple-element.40), kind=kOutput, calls=%fused_computation.12 | convolution fusion | flops 2151677952 | bytes 7341056 | tf_op jit(solution)/shard_map/rfl,slc->srfc/dot_general | solution.py:41
  27.5 0.0 copy-start
  27.5 1.3 copy-done
  28.8 0.0 copy-start.2
  28.8 1.4 dynamic-slice_bitcast_fusion.3
  30.2 1.1 copy.16
  31.3 3.5 %all-to-all-start = ((bf16[8,2,64,256]{3,0,1,2:T(8,128)(2,1)}), bf16[8,2,64,256]{3,0,1,2:T(8,128)(2,1)S(1)}, u32[]{:S(2)}, u32[]{:S(2)}) async-start(bf16[8,2,64,256]{3,0,1,2:T(8,128)(2,1)} %copy.16), calls=%async_computation | async-start | bytes 1048576 | tf_op jit(solution)/shard_map/all_to_all | solution.py:50
  34.8 1.1 copy.32
  35.9 6.3 %all-to-all-done = bf16[8,2,64,256]{3,0,1,2:T(8,128)(2,1)S(1)} async-done(((bf16[8,2,64,256]{3,0,1,2:T(8,128)(2,1)}), bf16[8,2,64,256]{3,0,1,2:T(8,128)(2,1)S(1)}, u32[]{:S(2)}, u32[]{:S(2)}) %all-to-all-start) | async-done | bytes 524320 | tf_op jit(solution)/shard_map/all_to_all | solution.py:50
  42.2 3.5 %all-to-all-start.6 = ((bf16[8,2,64,256]{3,0,1,2:T(8,128)(2,1)}), bf16[8,2,64,256]{3,0,1,2:T(8,128)(2,1)S(1)}, u32[]{:S(2)}, u32[]{:S(2)}) async-start(bf16[8,2,64,256]{3,0,1,2:T(8,128)(2,1)} %copy.32), calls=%async_computation.6 | async-start | bytes 1048576 | tf_op jit(solution)/shard_map/all_to_all | solution.py:57
  45.7 1.3 collective-permute-start.2
  47.0 1.1 copy.27
  48.1 4.2 %all-to-all-done.6 = bf16[8,2,64,256]{3,0,1,2:T(8,128)(2,1)S(1)} async-done(((bf16[8,2,64,256]{3,0,1,2:T(8,128)(2,1)}), bf16[8,2,64,256]{3,0,1,2:T(8,128)(2,1)S(1)}, u32[]{:S(2)}, u32[]{:S(2)}) %all-to-all-start.6) | async-done | bytes 524320 | tf_op jit(solution)/shard_map/all_to_all | solution.py:57
  52.3 3.5 %all-to-all-start.4 = ((bf16[8,2,64,256]{3,0,1,2:T(8,128)(2,1)}), bf16[8,2,64,256]{3,0,1,2:T(8,128)(2,1)S(1)}, u32[]{:S(2)}, u32[]{:S(2)}) async-start(bf16[8,2,64,256]{3,0,1,2:T(8,128)(2,1)} %copy.27), calls=%async_computation.4 | async-start | bytes 1048576 | tf_op jit(solution)/shard_map/all_to_all | solution.py:57
  55.8 4.8 %collective-permute-start.1 = (bf16[8,2,256,256]{3,2,0,1:T(8,128)(2,1)}, bf16[8,2,256,256]{3,2,0,1:T(8,128)(2,1)}, u32[]{:S(2)}, u32[]{:S(2)}) collective-permute-start(bf16[8,2,256,256]{3,2,0,1:T(8,128)(2,1)} %bitcast.184), channel_id=1, source_target_pairs={{4,0},{6,2},{8,4},{10,6},{12,8},{14,10},{16,12},{18,14},{20,16},{2... | collective-permute-start | bytes 6291464 | tf_op jit(solution)/shard_map/ppermute | solution.py:16
  60.6 0.0 collective-permute-start
  60.6 1.1 copy.22
  61.7 2.2 all-to-all-done.4
  63.9 3.5 %all-to-all-start.2 = ((bf16[8,2,64,256]{3,0,1,2:T(8,128)(2,1)}), bf16[8,2,64,256]{3,0,1,2:T(8,128)(2,1)S(1)}, u32[]{:S(2)}, u32[]{:S(2)}) async-start(bf16[8,2,64,256]{3,0,1,2:T(8,128)(2,1)} %copy.22), calls=%async_computation.2 | async-start | bytes 1048576 | tf_op jit(solution)/shard_map/all_to_all | solution.py:57
  67.4 0.0 copy-done.2
  67.4 0.7 fusion.44
  70.5 0.8 copy.49
  71.4 3.3 %all-to-all-done.2 = bf16[8,2,64,256]{3,0,1,2:T(8,128)(2,1)S(1)} async-done(((bf16[8,2,64,256]{3,0,1,2:T(8,128)(2,1)}), bf16[8,2,64,256]{3,0,1,2:T(8,128)(2,1)S(1)}, u32[]{:S(2)}, u32[]{:S(2)}) %all-to-all-start.2) | async-done | bytes 524320 | tf_op jit(solution)/shard_map/all_to_all | solution.py:57
  74.8 0.1 fusion.33
  74.9 1.1 slice_bitcast_fusion.1
  76.0 0.7 slice_bitcast_fusion.5
  76.8 13.5 %collective-permute-done.2 = bf16[8,2,256,256]{3,2,0,1:T(8,128)(2,1)} collective-permute-done((bf16[8,2,256,256]{3,2,0,1:T(8,128)(2,1)}, bf16[8,2,256,256]{3,2,0,1:T(8,128)(2,1)}, u32[]{:S(2)}, u32[]{:S(2)}) %collective-permute-start.2) | collective-permute-done | bytes 2097184 | tf_op jit(solution)/shard_map/ppermute | solution.py:16
  90.2 1.2 constant_dynamic-slice_fusion
  91.5 1.1 copy.29
  92.6 3.5 %all-to-all-start.5 = ((bf16[8,2,64,256]{3,0,1,2:T(8,128)(2,1)}), bf16[8,2,64,256]{3,0,1,2:T(8,128)(2,1)S(1)}, u32[]{:S(2)}, u32[]{:S(2)}) async-start(bf16[8,2,64,256]{3,0,1,2:T(8,128)(2,1)} %copy.29), calls=%async_computation.5 | async-start | bytes 1048576 | tf_op jit(solution)/shard_map/all_to_all | solution.py:58
  96.1 5.6 %fusion = bf16[1,2,32,256,256]{3,4,1,2,0:T(8,128)(2,1)} fusion(f32[]{:T(128)} %bitcast.15, bf16[16,32,256]{2,0,1:T(8,128)(2,1)S(1)} %get-tuple-element.9, bf16[16,32,256]{2,0,1:T(8,128)(2,1)S(1)} %get-tuple-element.10, bf16[1,32,32,256]{3,1,2,0:T(8,128)(2,1)S(1)} %get-tuple-element.24, bf16[1,32,32,256]{3,1,2,0:T(8,128)(2,1)S(1)} %get-tuple-element.23), kind=kOutput, calls=%fused_computation.6 | convolution fusion | flops 278396928 | bytes 9961476 | tf_op jit(solution)/shard_map/sfi,rsfj->rfij/dot_general | solution.py:32
  101.7 33.4 %collective-permute-done.1 = bf16[8,2,256,256]{3,2,0,1:T(8,128)(2,1)} collective-permute-done((bf16[8,2,256,256]{3,2,0,1:T(8,128)(2,1)}, bf16[8,2,256,256]{3,2,0,1:T(8,128)(2,1)}, u32[]{:S(2)}, u32[]{:S(2)}) %collective-permute-start.1) | collective-permute-done | bytes 2097184 | tf_op jit(solution)/shard_map/ppermute | solution.py:16
  135.2 1.2 constant_dynamic-slice_fusion.1
  136.4 1.1 copy.24
  137.5 23.2 %collective-permute-done = bf16[8,2,256,256]{3,2,0,1:T(8,128)(2,1)} collective-permute-done((bf16[8,2,256,256]{3,2,0,1:T(8,128)(2,1)}, bf16[8,2,256,256]{3,2,0,1:T(8,128)(2,1)}, u32[]{:S(2)}, u32[]{:S(2)}) %collective-permute-start) | collective-permute-done | bytes 2097184 | tf_op jit(solution)/shard_map/ppermute | solution.py:16
  160.7 1.2 constant_dynamic-slice_fusion.2
  162.0 1.1 copy.19
  163.1 0.0 all-to-all-done.5
  163.1 3.5 %all-to-all-start.3 = ((bf16[8,2,64,256]{3,0,1,2:T(8,128)(2,1)}), bf16[8,2,64,256]{3,0,1,2:T(8,128)(2,1)S(1)}, u32[]{:S(2)}, u32[]{:S(2)}) async-start(bf16[8,2,64,256]{3,0,1,2:T(8,128)(2,1)} %copy.24), calls=%async_computation.3 | async-start | bytes 1048576 | tf_op jit(solution)/shard_map/all_to_all | solution.py:58
  166.7 6.4 %all-to-all-done.3 = bf16[8,2,64,256]{3,0,1,2:T(8,128)(2,1)S(1)} async-done(((bf16[8,2,64,256]{3,0,1,2:T(8,128)(2,1)}), bf16[8,2,64,256]{3,0,1,2:T(8,128)(2,1)S(1)}, u32[]{:S(2)}, u32[]{:S(2)}) %all-to-all-start.3) | async-done | bytes 524320 | tf_op jit(solution)/shard_map/all_to_all | solution.py:58
  173.1 3.7 %all-to-all-start.1 = ((bf16[8,2,64,256]{3,0,1,2:T(8,128)(2,1)}), bf16[8,2,64,256]{3,0,1,2:T(8,128)(2,1)S(1)}, u32[]{:S(2)}, u32[]{:S(2)}) async-start(bf16[8,2,64,256]{3,0,1,2:T(8,128)(2,1)} %copy.19), calls=%async_computation.1 | async-start | bytes 1048576 | tf_op jit(solution)/shard_map/all_to_all | solution.py:58
  176.9 0.7 slice_bitcast_fusion.6
  177.6 5.6 %all-to-all-done.1 = bf16[8,2,64,256]{3,0,1,2:T(8,128)(2,1)S(1)} async-done(((bf16[8,2,64,256]{3,0,1,2:T(8,128)(2,1)}), bf16[8,2,64,256]{3,0,1,2:T(8,128)(2,1)S(1)}, u32[]{:S(2)}, u32[]{:S(2)}) %all-to-all-start.1) | async-done | bytes 524320 | tf_op jit(solution)/shard_map/all_to_all | solution.py:58
  183.3 0.0 copy-start.1
  183.3 0.1 maximum_bitcast_fusion.12
  183.4 1.2 maximum_bitcast_fusion.8
  184.6 0.1 maximum_bitcast_fusion.4
  184.7 5.6 %fusion.1 = bf16[1,2,32,256,256]{3,4,1,2,0:T(8,128)(2,1)} fusion(f32[]{:T(128)} %bitcast.38, bf16[1,32,32,256]{3,1,0,2:T(8,128)(2,1)S(1)} %get-tuple-element.26, bf16[1,32,32,256]{3,1,0,2:T(8,128)(2,1)S(1)} %get-tuple-element.25, bf16[16,32,256]{2,0,1:T(8,128)(2,1)S(1)} %get-tuple-element.12, bf16[16,32,256]{2,0,1:T(8,128)(2,1)S(1)} %get-tuple-element.11), kind=kOutput, calls=%fused_computation.7 | convolution fusion | flops 278396928 | bytes 9961476 | tf_op jit(solution)/shard_map/sfi,rsfj->rfij/dot_general | solution.py:32
  190.3 0.0 copy-done.1
  190.3 5.6 %fusion.2 = bf16[1,2,32,256,256]{3,4,1,2,0:T(8,128)(2,1)} fusion(f32[]{:T(128)} %bitcast.60, bf16[1,32,32,256]{3,1,0,2:T(8,128)(2,1)S(1)} %get-tuple-element.28, bf16[1,32,32,256]{3,1,0,2:T(8,128)(2,1)S(1)} %get-tuple-element.27, bf16[16,32,256]{2,0,1:T(8,128)(2,1)S(1)} %copy-done.1, bf16[16,32,256]{2,0,1:T(8,128)(2,1)S(1)} %get-tuple-element.15), kind=kOutput, calls=%fused_computation.8 | convolution fusion | flops 278396928 | bytes 9961476 | tf_op jit(solution)/shard_map/sfi,rsfj->rfij/dot_general | solution.py:32
  195.9 5.8 %fusion.3 = bf16[1,2,32,256,256]{3,4,1,2,0:T(8,128)(2,1)} fusion(f32[]{:T(128)} %bitcast.82, bf16[1,32,32,256]{3,1,0,2:T(8,128)(2,1)S(1)} %get-tuple-element.30, bf16[1,32,32,256]{3,1,0,2:T(8,128)(2,1)S(1)} %get-tuple-element.29, bf16[16,32,256]{2,0,1:T(8,128)(2,1)S(1)} %get-tuple-element.20, bf16[16,32,256]{2,0,1:T(8,128)(2,1)S(1)} %get-tuple-element.19), kind=kOutput, calls=%fused_computation.9 | convolution fusion | flops 278396928 | bytes 9961476 | tf_op jit(solution)/shard_map/sfi,rsfj->rfij/dot_general | solution.py:32
  201.7 22.7 %maximum_bitcast_fusion = bf16[1,4,2,32,256,256]{4,5,2,3,1,0:T(8,128)(2,1)} fusion(bf16[1,2,32,256,256]{3,4,1,2,0:T(8,128)(2,1)} %fusion.3, bf16[1,2,32,256,256]{3,4,1,2,0:T(8,128)(2,1)} %fusion.2, bf16[1,2,32,256,256]{3,4,1,2,0:T(8,128)(2,1)} %fusion.1, bf16[1,2,32,256,256]{3,4,1,2,0:T(8,128)(2,1)} %fusion), kind=kLoop, calls=%fused_computation | loop fusion | flops 50331648 | bytes 67108864 | tf_op jit(solution)/shard_map/broadcast_in_dim | solution.py:63
  224.4 40.5 %copy.34 = bf16[1,4,2,32,256,256]{5,4,3,2,1,0:T(8,128)(2,1)} copy(bf16[1,4,2,32,256,256]{4,5,2,3,1,0:T(8,128)(2,1)} %maximum_bitcast_fusion) | data formatting | bytes 67108864 | tf_op jit(solution)/shard_map/broadcast_in_dim | solution.py:63
  (17 shorter events, 0.5 us)
Async XLA Ops:
  27.5 1.3 copy-start
  28.8 38.5 %copy-start.2 = (s32[1,4]{1,0:T(1,128)S(1)}, s32[1,4]{1,0:T(1,128)}, u32[]{:S(2)}) copy-start(s32[1,4]{1,0:T(1,128)} %param.5) | copy-start | bytes 52
  31.3 10.9 %all-to-all-start = ((bf16[8,2,64,256]{3,0,1,2:T(8,128)(2,1)}), bf16[8,2,64,256]{3,0,1,2:T(8,128)(2,1)S(1)}, u32[]{:S(2)}, u32[]{:S(2)}) async-start(bf16[8,2,64,256]{3,0,1,2:T(8,128)(2,1)} %copy.16), calls=%async_computation | async-start | bytes 1048576 | tf_op jit(solution)/shard_map/all_to_all | solution.py:50
  42.2 10.1 %all-to-all-start.6 = ((bf16[8,2,64,256]{3,0,1,2:T(8,128)(2,1)}), bf16[8,2,64,256]{3,0,1,2:T(8,128)(2,1)S(1)}, u32[]{:S(2)}, u32[]{:S(2)}) async-start(bf16[8,2,64,256]{3,0,1,2:T(8,128)(2,1)} %copy.32), calls=%async_computation.6 | async-start | bytes 1048576 | tf_op jit(solution)/shard_map/all_to_all | solution.py:57
  45.7 44.5 %collective-permute-start.2 = (bf16[8,2,256,256]{3,2,0,1:T(8,128)(2,1)}, bf16[8,2,256,256]{3,2,0,1:T(8,128)(2,1)}, u32[]{:S(2)}, u32[]{:S(2)}) collective-permute-start(bf16[8,2,256,256]{3,2,0,1:T(8,128)(2,1)} %bitcast.183), channel_id=1, source_target_pairs={{6,0},{8,2},{10,4},{12,6},{14,8},{16,10},{18,12},{20,14},{22,16},{... | collective-permute-start | bytes 6291464 | tf_op jit(solution)/shard_map/ppermute | solution.py:16
  52.3 11.6 %all-to-all-start.4 = ((bf16[8,2,64,256]{3,0,1,2:T(8,128)(2,1)}), bf16[8,2,64,256]{3,0,1,2:T(8,128)(2,1)S(1)}, u32[]{:S(2)}, u32[]{:S(2)}) async-start(bf16[8,2,64,256]{3,0,1,2:T(8,128)(2,1)} %copy.27), calls=%async_computation.4 | async-start | bytes 1048576 | tf_op jit(solution)/shard_map/all_to_all | solution.py:57
  55.8 79.4 %collective-permute-start.1 = (bf16[8,2,256,256]{3,2,0,1:T(8,128)(2,1)}, bf16[8,2,256,256]{3,2,0,1:T(8,128)(2,1)}, u32[]{:S(2)}, u32[]{:S(2)}) collective-permute-start(bf16[8,2,256,256]{3,2,0,1:T(8,128)(2,1)} %bitcast.184), channel_id=1, source_target_pairs={{4,0},{6,2},{8,4},{10,6},{12,8},{14,10},{16,12},{18,14},{20,16},{2... | collective-permute-start | bytes 6291464 | tf_op jit(solution)/shard_map/ppermute | solution.py:16
  60.6 100.1 %collective-permute-start = (bf16[8,2,256,256]{3,2,0,1:T(8,128)(2,1)}, bf16[8,2,256,256]{3,2,0,1:T(8,128)(2,1)}, u32[]{:S(2)}, u32[]{:S(2)}) collective-permute-start(bf16[8,2,256,256]{3,2,0,1:T(8,128)(2,1)} %bitcast.185), channel_id=1, source_target_pairs={{2,0},{4,2},{6,4},{8,6},{10,8},{12,10},{14,12},{16,14},{18,16},{20... | collective-permute-start | bytes 6291464 | tf_op jit(solution)/shard_map/ppermute | solution.py:16
  63.9 10.8 %all-to-all-start.2 = ((bf16[8,2,64,256]{3,0,1,2:T(8,128)(2,1)}), bf16[8,2,64,256]{3,0,1,2:T(8,128)(2,1)S(1)}, u32[]{:S(2)}, u32[]{:S(2)}) async-start(bf16[8,2,64,256]{3,0,1,2:T(8,128)(2,1)} %copy.22), calls=%async_computation.2 | async-start | bytes 1048576 | tf_op jit(solution)/shard_map/all_to_all | solution.py:57
  92.6 70.5 %all-to-all-start.5 = ((bf16[8,2,64,256]{3,0,1,2:T(8,128)(2,1)}), bf16[8,2,64,256]{3,0,1,2:T(8,128)(2,1)S(1)}, u32[]{:S(2)}, u32[]{:S(2)}) async-start(bf16[8,2,64,256]{3,0,1,2:T(8,128)(2,1)} %copy.29), calls=%async_computation.5 | async-start | bytes 1048576 | tf_op jit(solution)/shard_map/all_to_all | solution.py:58
  163.1 10.1 %all-to-all-start.3 = ((bf16[8,2,64,256]{3,0,1,2:T(8,128)(2,1)}), bf16[8,2,64,256]{3,0,1,2:T(8,128)(2,1)S(1)}, u32[]{:S(2)}, u32[]{:S(2)}) async-start(bf16[8,2,64,256]{3,0,1,2:T(8,128)(2,1)} %copy.24), calls=%async_computation.3 | async-start | bytes 1048576 | tf_op jit(solution)/shard_map/all_to_all | solution.py:58
  173.1 10.1 %all-to-all-start.1 = ((bf16[8,2,64,256]{3,0,1,2:T(8,128)(2,1)}), bf16[8,2,64,256]{3,0,1,2:T(8,128)(2,1)S(1)}, u32[]{:S(2)}, u32[]{:S(2)}) async-start(bf16[8,2,64,256]{3,0,1,2:T(8,128)(2,1)} %copy.19), calls=%async_computation.1 | async-start | bytes 1048576 | tf_op jit(solution)/shard_map/all_to_all | solution.py:58
  183.3 7.0 %copy-start.1 = (bf16[16,32,256]{2,0,1:T(8,128)(2,1)S(1)}, bf16[16,32,256]{2,0,1:T(8,128)(2,1)}, u32[]{:S(2)}) copy-start(bf16[16,32,256]{2,0,1:T(8,128)(2,1)} %get-tuple-element.16) | copy-start | bytes 786436
where the time goes:
time: 267 us; the launch traced here: 265 us
  waiting for transfers between devices  98.1 us (37%)
  local copies, waits for them, and re-layouts  60.5 us (23%)
  other arithmetic  32.1 us (12%)
  starting transfers between devices  30.7 us (11%)
  matrix products  27.2 us (10%)
  between operations  10.5 us (4%)
  blocking collectives  5.83 us (2%)
    ppermute x3, waiting for transfers between devices, from_behind(): return lax.ppermute(block, axis, route)  70.1 us
    broadcast_in_dim x1, local copies, waits for them, and re-layouts, body(): return jnp.stack(results)[None]  40.5 us
    broadcast_in_dim x1, other arithmetic, body(): return jnp.stack(results)[None]  22.7 us
    dot_general x4, matrix products, pair_cross(): jnp.einsum('sfi,rsfj->rfij', stacked, partner, preferred_element_type=jnp...  22.6 us
    all_to_all x4, waiting for transfers between devices, body(): lax.all_to_all(own, 'seg', split_axis=2, concat_axis=0, tiled=True)  15.9 us
    all_to_all x4, starting transfers between devices, body(): lax.all_to_all(own, 'seg', split_axis=2, concat_axis=0, tiled=True)  13.9 us
    all_to_all x3, waiting for transfers between devices, body(): lax.all_to_all(other, 'seg', split_axis=2, concat_axis=0, tiled=True)  12 us
    all_to_all x3, starting transfers between devices, body(): lax.all_to_all(other, 'seg', split_axis=2, concat_axis=0, tiled=True)  10.6 us
  transfers between devices with their start and end apart: 10, of which 9 were waited for; matrix products, arithmetic and copies ran while one was open for 8% of the time, Pallas kernels for 0%

commit v1 on v0

v1 whole, which is shorter than its diff:
```python
import functools

import jax
import jax.numpy as jnp
import ml_dtypes
import numpy as np
from jax import lax
from jax.experimental import pallas as pl
from jax.experimental.pallas import tpu as pltpu
from jax.sharding import PartitionSpec as P

NB = 256
BW = 64
PAIRS = 4
LANES = 128
LIFT = 1024.0


def dft_table(nbins, length):
    freq = np.arange(nbins)[:, None]
    sample = np.arange(length)[None, :]
    phase = (freq * sample % length) * (2.0 * np.pi / length)
    window = 0.5 - 0.5 * np.cos(sample * (2.0 * np.pi / length))
    table = np.concatenate([window * np.cos(phase), -window * np.sin(phase)])
    return (table.astype(np.float32).astype(ml_dtypes.bfloat16).astype(np.float32) * LIFT).astype(ml_dtypes.bfloat16)


def window_plan(seg):
    own = [(pair, False, shift) for pair in range(PAIRS) for shift in range(seg)]
    lent = [(pair, True, shift) for pair in range(1, PAIRS) for shift in range(seg)]
    return sorted(own + lent, key=lambda w: (w[0], -w[2], w[1]))


def carries_power(window):
    pair, lent, _ = window
    return lent or pair == 0


def split3(x):
    high = x.astype(jnp.bfloat16)
    rest = x - high.astype(jnp.float32)
    mid = rest.astype(jnp.bfloat16)
    low = (rest - mid.astype(jnp.float32)).astype(jnp.bfloat16)
    return high, mid, low


def spectra_kernel(plan, chan, seg, band_ref, table_hbm, signal_hbm, *refs):
    n = len(plan)
    outs, (table, signal, raw, cut, table_sem, signal_sem, out_sem) = refs[:n], refs[n:]
    segs, _, width = signal.shape
    nbins = table.shape[0] // 2
    rows = 2 * segs
    bins = BW // seg
    table_copy = pltpu.make_async_copy(table_hbm, table, table_sem)
    signal_copy = pltpu.make_async_copy(signal_hbm, signal, signal_sem)
    table_copy.start()
    signal_copy.start()
    block, seat = lax.axis_index("chan"), lax.axis_index("seg")
    table_copy.wait()
    signal_copy.wait()
    power = jnp.zeros((8, width), jnp.float32)
    for s in range(segs):
        spectrum = jnp.dot(table[...], signal[s], preferred_element_type=jnp.float32)
        for r in range(2):
            for h in range(width // LANES):
                raw[h, pl.ds(r * segs + s, nbins, stride=rows), :] = spectrum[r * nbins : (r + 1) * nbins, h * LANES : (h + 1) * LANES]
        x = signal[s].astype(jnp.float32)
        power = power + jnp.sum((x * x).reshape(-1, 8, width), axis=0)
    parts = split3(jnp.sum(power, axis=0, keepdims=True))
    row = lax.broadcasted_iota(jnp.int32, (rows, width), 0)
    packed = jnp.zeros((rows, width), jnp.float32)
    for i, part in enumerate(parts):
        packed = jnp.where(row == i, part.astype(jnp.float32), packed)
    packed = packed.astype(jnp.bfloat16)
    copies = []
    for k, (pair, lent, shift) in enumerate(plan):
        user = lax.rem(block + (chan - pair), chan) if lent else block
        first = band_ref[user, pair] + lax.rem(seat + shift, seg) * bins
        start = pl.multiple_of(first * rows, rows)
        for h in range(width // LANES):
            piece = raw[h, pl.ds(start, bins * rows), :].reshape(bins, rows, LANES)
            cut[k, :bins, :, h * LANES : (h + 1) * LANES] = piece.astype(jnp.bfloat16)
        size = bins
        if carries_power(plan[k]):
            cut[k, bins] = packed
            size = bins + 1
        copy = pltpu.make_async_copy(cut.at[k, pl.ds(0, size)], outs[k], out_sem.at[k])
        copy.start()
        copies.append(copy)
    for copy in copies:
        copy.wait()


def cut_spectra(plan, chan, seg, band, table, signal):
    segs, length, width = signal.shape
    rows, bins, n = 2 * segs, BW // seg, len(plan)
    anywhere = pl.BlockSpec(memory_space=pl.ANY)
    return pl.pallas_call(
        functools.partial(spectra_kernel, plan, chan, seg),
        in_specs=[pl.BlockSpec(memory_space=pltpu.SMEM), anywhere, anywhere],
        out_specs=[anywhere] * n,
        out_shape=[jax.ShapeDtypeStruct((bins + carries_power(w), rows, width), jnp.bfloat16) for w in plan],
        scratch_shapes=[
            pltpu.VMEM(table.shape, jnp.bfloat16),
            pltpu.VMEM(signal.shape, jnp.bfloat16),
            pltpu.VMEM((width // LANES, table.shape[0] * segs, LANES), jnp.float32),
            pltpu.VMEM((n, bins + 1, rows, width), jnp.bfloat16),
            pltpu.SemaphoreType.DMA,
            pltpu.SemaphoreType.DMA,
            pltpu.SemaphoreType.DMA((n,)),
        ],
        compiler_params=pltpu.CompilerParams(vmem_limit_bytes=56 << 20),
    )(band, table, signal)


def turned(x):
    half = x.shape[1] // 2
    return jnp.concatenate([x[:, half:], -x[:, :half]], axis=1)


def inv_rms_of(tiles, samples):
    power = 0.0
    for tile in tiles:
        t = tile[0].astype(jnp.float32)
        power = power + (t[0:1] + t[1:2] + t[2:3])
    return lax.rsqrt(power / samples + 1e-06)


def cross_kernel(pair, seg, samples, scale, sched_ref, *refs):
    mine, theirs = refs[:seg], refs[seg : 2 * seg]
    my_power, their_power = refs[2 * seg : 3 * seg], refs[3 * seg : 4 * seg]
    out, by_row, by_column = refs[-3:]
    bins, _, width = mine[0].shape
    live = sched_ref[0, pair]

    @pl.when(live == 0)
    def _():
        out[...] = jnp.zeros(out.shape, out.dtype)

    @pl.when((live != 0) & (pl.program_id(0) == 0))
    def _():
        by_row[...] = jnp.broadcast_to(inv_rms_of(my_power, samples) * scale, (width, width)).T
        by_column[...] = inv_rms_of(their_power, samples)

    @pl.when(live != 0)
    def _():
        for f in range(bins):
            x = jnp.concatenate([m[f] for m in mine], axis=0)
            xt = jnp.concatenate([turned(m[f : f + 1])[0] for m in mine], axis=0)
            y = jnp.concatenate([t[f] for t in theirs], axis=0)
            for r, first in enumerate((x, xt)):
                product = lax.dot_general(first, y, (((0,), (0,)), ((), ())), preferred_element_type=jnp.float32)
                out[0, 0, r, f] = (product * by_row[...] * by_column[...]).astype(out.dtype)


def cross(pair, seg, samples, scale, sched, mine, theirs, my_power, their_power, shape, out):
    rows, width = mine[0].shape[1:]
    total = shape[3]
    bins = min(16, total)
    block = pl.BlockSpec((bins, rows, width), lambda i, sched: (i, 0, 0))
    tile = pl.BlockSpec((1, rows, width), lambda i, sched: (total, 0, 0))
    operands = [sched, *mine, *theirs, *my_power, *their_power]
    in_specs = [block] * (2 * seg) + [tile] * (2 * seg)
    aliases = {}
    if out is not None:
        aliases = {len(operands): 0}
        operands.append(out)
        in_specs.append(pl.BlockSpec(memory_space=pl.ANY))
    return pl.pallas_call(
        functools.partial(cross_kernel, pair, seg, samples, scale),
        grid_spec=pltpu.PrefetchScalarGridSpec(
            num_scalar_prefetch=1,
            grid=(total // bins,),
            in_specs=in_specs,
            out_specs=pl.BlockSpec((1, 1, 2, bins, width, width), lambda i, sched: (0, pair, 0, i, 0, 0)),
            scratch_shapes=[pltpu.VMEM((width, width), jnp.float32), pltpu.VMEM((1, width), jnp.float32)],
        ),
        out_shape=jax.ShapeDtypeStruct(shape, jnp.bfloat16),
        input_output_aliases=aliases,
        compiler_params=pltpu.CompilerParams(vmem_limit_bytes=56 << 20),
        cost_estimate=pl.CostEstimate(
            flops=4 * total * seg * rows * width * width, bytes_accessed=4 * total * width * width, transcendentals=0
        ),
    )(*operands)


def body(signal, band, sched):
    seg_dev, length, width = signal.shape
    seg, chan = lax.axis_size("seg"), lax.axis_size("chan")
    segs = seg_dev * seg
    plan = window_plan(seg)
    table = jnp.asarray(dft_table(NB, length))
    cuts = dict(zip(plan, cut_spectra(plan, chan, seg, band, table, signal)))

    def delivered(window):
        pair, lent, shift = window
        away = pair if lent else 0
        if not away and not shift:
            return cuts[window]
        route = [(c * seg + s, (c - away) % chan * seg + (s + shift) % seg) for c in range(chan) for s in range(seg)]
        return lax.ppermute(cuts[window], ("chan", "seg"), route)

    arrived = {window: delivered(window) for window in plan}
    scale = 1.0 / (segs * 0.375 * length) / LIFT**2
    shape = (1, PAIRS, 2, BW // seg, width, width)
    my_power = [arrived[0, False, k] for k in range(seg)]
    out = None
    for pair in range(PAIRS):
        mine = [arrived[pair, False, k] for k in range(seg)]
        theirs = [arrived[pair, True, k] for k in range(seg)] if pair else mine
        their_power = theirs if pair else my_power
        out = cross(pair, seg, segs * length, scale, sched, mine, theirs, my_power, their_power, shape, out)
    return out


def solution(mesh):
    in_specs = (P("seg", None, "chan"), P(), P("chan", None))
    out_specs = P("chan", None, None, "seg", None, None)
    return jax.shard_map(body, mesh=mesh, in_specs=in_specs, out_specs=out_specs, check_vma=False)
```

time: 267 us -> 71.8 us (0.27)
  the two profiles are of different devices: /device:TPU:0 before, /device:TPU:4 now
where the time goes in v1:
time: 71.8 us; the launch traced here: 70.7 us
  Pallas kernels  32.7 us (46%)
  starting transfers between devices  22 us (31%)
  waiting for transfers between devices  12.9 us (18%)
  local copies, waits for them, and re-layouts  2.98 us (4%)
    pallas_call x4, Pallas kernels, cross(): pl.pallas_call(functools.partial(cross_kernel, pair, seg, samples, scale)...  24.2 us
    ppermute x10, starting transfers between devices, delivered(): return lax.ppermute(cuts[window], ('chan', 'seg'), route)  22 us
    ppermute x10, waiting for transfers between devices, delivered(): return lax.ppermute(cuts[window], ('chan', 'seg'), route)  12.9 us
    pallas_call x1, Pallas kernels, cut_spectra(): pl.pallas_call(functools.partial(spectra_kernel, plan, chan, seg), in_spe...  8.51 us
    unnamed x21, local copies, waits for them, and re-layouts  2.98 us
  transfers between devices with their start and end apart: 10, of which 3 were waited for; matrix products, arithmetic and copies ran while one was open for 0% of the time, Pallas kernels for 27%

profile of v1, /device:TPU:4, one launch (start us, length us, event | category | flops | bytes accessed | tf_op | source)
XLA Modules:
  0.0 70.7 jit_solution(5969735510179806391)
XLA Ops:
  0.0 1.3 %copy.8.band_ref = s32[16,4]{1,0:T(8,128)} copy(s32[16,4]{0,1:T(4,128)} %param.5) | data formatting | bytes 512 | tf_op args[1]
  1.3 8.5 %shard_map.46 = (bf16[33,16,256]{2,1,0:T(8,128)(2,1)}, bf16[33,16,256]{2,1,0:T(8,128)(2,1)}, bf16[32,16,256]{2,1,0:T(8,128)(2,1)}, bf16[33,16,256]{2,1,0:T(8,128...) custom-call(s32[16,4]{1,0:T(8,128)} %copy.8.band_ref, ...), custom_call_target="tpu_custom_call" | custom-call | tf_op jit(solution)/shard_map/pallas_call | solution.py:98
  9.9 1.6 %collective-permute-start.4 = (bf16[32,16,256]{2,1,0:T(8,128)(2,1)}, bf16[32,16,256]{2,1,0:T(8,128)(2,1)S(1)}, u32[]{:S(2)}, u32[]{:S(2)}) collective-permute-start(bf16[32,16,256]{2,1,0:T(8,128)(2,1)} %get-tuple-element.26), channel_id=1, source_target_pairs={{0,1},{1,0},{2,3},{3,2},{4,5},{5,4},{6,7},{7,6},{8,9},{9,8},{10,11... | collective-permute-start | bytes 786440 | tf_op jit(solution)/shard_map/ppermute | solution.py:201
  11.4 0.5 collective-permute-start.7
  12.0 1.5 %collective-permute-start.3 = (bf16[33,16,256]{2,1,0:T(8,128)(2,1)}, bf16[33,16,256]{2,1,0:T(8,128)(2,1)S(1)}, u32[]{:S(2)}, u32[]{:S(2)}) collective-permute-start(bf16[33,16,256]{2,1,0:T(8,128)(2,1)} %get-tuple-element.24), channel_id=1, source_target_pairs={{0,1},{1,0},{2,3},{3,2},{4,5},{5,4},{6,7},{7,6},{8,9},{9,8},{10,11... | collective-permute-start | bytes 811016 | tf_op jit(solution)/shard_map/ppermute | solution.py:201
  13.4 0.0 collective-permute-start.8
  13.4 0.1 collective-permute-start.9
  13.6 5.8 %collective-permute-done.4.refs_1_ = bf16[32,16,256]{2,1,0:T(8,128)(2,1)S(1)} collective-permute-done((bf16[32,16,256]{2,1,0:T(8,128)(2,1)}, bf16[32,16,256]{2,1,0:T(8,128)(2,1)S(1)}, u32[]{:S(2)}, u32[]{:S(2)}) %collective-permute-start.4) | collective-permute-done | bytes 262176 | tf_op jit(solution)/shard_map/ppermute | solution.py:201
  19.3 0.0 copy-start.7
  19.3 0.0 collective-permute-start.5
  19.3 5.6 %collective-permute-done.7.refs_1_ = bf16[32,16,256]{2,1,0:T(8,128)(2,1)S(1)} collective-permute-done((bf16[32,16,256]{2,1,0:T(8,128)(2,1)}, bf16[32,16,256]{2,1,0:T(8,128)(2,1)S(1)}, u32[]{:S(2)}, u32[]{:S(2)}) %collective-permute-start.7) | collective-permute-done | bytes 262176 | tf_op jit(solution)/shard_map/ppermute | solution.py:201
  25.0 0.0 copy-start.8
  25.0 4.3 %collective-permute-start.6 = (bf16[33,16,256]{2,1,0:T(8,128)(2,1)}, bf16[33,16,256]{2,1,0:T(8,128)(2,1)S(1)}, u32[]{:S(2)}, u32[]{:S(2)}) collective-permute-start(bf16[33,16,256]{2,1,0:T(8,128)(2,1)} %get-tuple-element.28), channel_id=1, source_target_pairs={{0,29},{1,28},{2,31},{3,30},{4,1},{5,0},{6,3},{7,2},{8,5},{9,4},{1... | collective-permute-start | bytes 811016 | tf_op jit(solution)/shard_map/ppermute | solution.py:201
  29.3 1.5 %collective-permute-done.3.refs_1_.refs_3_.refs_5_.refs_7_ = bf16[33,16,256]{2,1,0:T(8,128)(2,1)S(1)} collective-permute-done((bf16[33,16,256]{2,1,0:T(8,128)(2,1)}, bf16[33,16,256]{2,1,0:T(8,128)(2,1)S(1)}, u32[]{:S(2)}, u32[]{:S(2)}) %collective-permute-start.3) | collective-permute-done | bytes 270368 | tf_op jit(solution)/shard_map/ppermute | solution.py:201
  30.8 0.0 copy-start
  30.8 1.0 %collective-permute-start.1 = (bf16[33,16,256]{2,1,0:T(8,128)(2,1)}, bf16[33,16,256]{2,1,0:T(8,128)(2,1)S(1)}, u32[]{:S(2)}, u32[]{:S(2)}) collective-permute-start(bf16[33,16,256]{2,1,0:T(8,128)(2,1)} %get-tuple-element.21), channel_id=1, source_target_pairs={{0,26},{1,27},{2,28},{3,29},{4,30},{5,31},{6,0},{7,1},{8,2},{9,3},... | collective-permute-start | bytes 811016 | tf_op jit(solution)/shard_map/ppermute | solution.py:201
  31.8 0.0 collective-permute-done.8.refs_2_.refs_6_
  31.8 0.0 copy-start.3
  31.8 12.4 %collective-permute-start.2 = (bf16[33,16,256]{2,1,0:T(8,128)(2,1)}, bf16[33,16,256]{2,1,0:T(8,128)(2,1)S(1)}, u32[]{:S(2)}, u32[]{:S(2)}) collective-permute-start(bf16[33,16,256]{2,1,0:T(8,128)(2,1)} %get-tuple-element.22), channel_id=1, source_target_pairs={{0,27},{1,26},{2,29},{3,28},{4,31},{5,30},{6,1},{7,0},{8,3},{9,2},... | collective-permute-start | bytes 811016 | tf_op jit(solution)/shard_map/ppermute | solution.py:201
  44.2 0.0 collective-permute-done.9.refs_3_.refs_7_
  44.2 0.0 copy-start.5
  44.2 0.5 collective-permute-start
  44.7 0.0 copy-done
  44.8 5.6 %shard_map.47.refs_8_ = bf16[1,4,2,32,256,256]{5,4,3,2,1,0:T(8,128)(2,1)} custom-call(s32[1,4]{1,0:T(1,128)} %sched_ref.7, bf16[33,16,256]{2,1,0:T(8,128)(2,1)} %get-tuple-element.23.refs_0_.refs_2_.refs_4_.refs_6_, bf16[33,16,256]{2,1,0:T(8,128)(2,1)} %copy-done, bf16[33,16,256]{2,1,0:T(8,128)(2,1)} %get-tuple-element.23.refs_0_.refs_2_.refs_4_.refs_6_, ...), custom_call_target="tpu_custom_call" | custom-call | flops 268435456 | bytes 8388608 | tf_op jit(solution)/shard_map/pallas_call | solution.py:169
  50.3 0.0 copy-done.8
  50.3 0.0 copy-done.3
  50.3 0.0 copy-done.5
  50.3 6.6 %shard_map.48.refs_8_ = bf16[1,4,2,32,256,256]{5,4,3,2,1,0:T(8,128)(2,1)} custom-call(s32[1,4]{1,0:T(1,128)} %sched_ref.7, bf16[32,16,256]{2,1,0:T(8,128)(2,1)} %get-tuple-element.29.refs_0_, bf16[32,16,256]{2,1,0:T(8,128)(2,1)} %copy-done.8, bf16[33,16,256]{2,1,0:T(8,128)(2,1)} %copy-done.3, ...), custom_call_target="tpu_custom_call", output_to_operand_aliasing={{}: (9, {})} | custom-call | flops 268435456 | bytes 8388608 | tf_op jit(solution)/shard_map/pallas_call | solution.py:169
  56.9 0.0 collective-permute-done.5.refs_2_.refs_6_
  56.9 0.0 copy-start.2
  56.9 0.0 collective-permute-done.6.refs_3_.refs_7_
  57.0 0.0 copy-start.6
  57.0 0.0 copy-done.7
  57.0 0.7 copy-done.2
  57.6 0.1 copy-done.6
  57.7 6.6 %shard_map.49.refs_8_ = bf16[1,4,2,32,256,256]{5,4,3,2,1,0:T(8,128)(2,1)} custom-call(s32[1,4]{1,0:T(1,128)} %sched_ref.7, bf16[32,16,256]{2,1,0:T(8,128)(2,1)} %get-tuple-element.25.refs_0_, bf16[32,16,256]{2,1,0:T(8,128)(2,1)} %copy-done.7, bf16[33,16,256]{2,1,0:T(8,128)(2,1)} %copy-done.2, ...), custom_call_target="tpu_custom_call", output_to_operand_aliasing={{}: (9, {})} | custom-call | flops 268435456 | bytes 8388608 | tf_op jit(solution)/shard_map/pallas_call | solution.py:169
  64.3 0.0 collective-permute-done.refs_1_
  64.3 0.0 copy-start.9
  64.4 0.0 collective-permute-done.1.refs_2_.refs_6_
  64.4 0.0 copy-start.1
  64.4 0.0 collective-permute-done.2.refs_3_.refs_7_
  64.4 0.0 copy-start.4
  64.4 0.7 copy-done.9
  65.0 0.1 copy-done.1
  65.1 0.1 copy-done.4
  65.2 5.5 %shard_map.50 = bf16[1,4,2,32,256,256]{5,4,3,2,1,0:T(8,128)(2,1)} custom-call(s32[1,4]{1,0:T(1,128)} %sched_ref.7, bf16[32,16,256]{2,1,0:T(8,128)(2,1)} %get-tuple-element.19.refs_0_, bf16[32,16,256]{2,1,0:T(8,128)(2,1)} %copy-done.9, bf16[33,16,256]{2,1,0:T(8,128)(2,1)} %copy-done.1, ...), custom_call_target="tpu_custom_call", output_to_operand_aliasing={{}: (9, {})} | custom-call | flops 268435456 | bytes 8388608 | tf_op jit(solution)/shard_map/pallas_call | solution.py:169
Async XLA Ops:
  9.9 9.5 %collective-permute-start.4 = (bf16[32,16,256]{2,1,0:T(8,128)(2,1)}, bf16[32,16,256]{2,1,0:T(8,128)(2,1)S(1)}, u32[]{:S(2)}, u32[]{:S(2)}) collective-permute-start(bf16[32,16,256]{2,1,0:T(8,128)(2,1)} %get-tuple-element.26), channel_id=1, source_target_pairs={{0,1},{1,0},{2,3},{3,2},{4,5},{5,4},{6,7},{7,6},{8,9},{9,8},{10,11... | collective-permute-start | bytes 786440 | tf_op jit(solution)/shard_map/ppermute | solution.py:201
  11.4 13.5 %collective-permute-start.7 = (bf16[32,16,256]{2,1,0:T(8,128)(2,1)}, bf16[32,16,256]{2,1,0:T(8,128)(2,1)S(1)}, u32[]{:S(2)}, u32[]{:S(2)}) collective-permute-start(bf16[32,16,256]{2,1,0:T(8,128)(2,1)} %get-tuple-element.30), channel_id=1, source_target_pairs={{0,1},{1,0},{2,3},{3,2},{4,5},{5,4},{6,7},{7,6},{8,9},{9,8},{10,11... | collective-permute-start | bytes 786440 | tf_op jit(solution)/shard_map/ppermute | solution.py:201
  12.0 18.8 %collective-permute-start.3 = (bf16[33,16,256]{2,1,0:T(8,128)(2,1)}, bf16[33,16,256]{2,1,0:T(8,128)(2,1)S(1)}, u32[]{:S(2)}, u32[]{:S(2)}) collective-permute-start(bf16[33,16,256]{2,1,0:T(8,128)(2,1)} %get-tuple-element.24), channel_id=1, source_target_pairs={{0,1},{1,0},{2,3},{3,2},{4,5},{5,4},{6,7},{7,6},{8,9},{9,8},{10,11... | collective-permute-start | bytes 811016 | tf_op jit(solution)/shard_map/ppermute | solution.py:201
  13.4 18.3 %collective-permute-start.8 = (bf16[33,16,256]{2,1,0:T(8,128)(2,1)}, bf16[33,16,256]{2,1,0:T(8,128)(2,1)S(1)}, u32[]{:S(2)}, u32[]{:S(2)}) collective-permute-start(bf16[33,16,256]{2,1,0:T(8,128)(2,1)} %get-tuple-element.31), channel_id=1, source_target_pairs={{0,30},{1,31},{2,0},{3,1},{4,2},{5,3},{6,4},{7,5},{8,6},{9,7},{10,... | collective-permute-start | bytes 811016 | tf_op jit(solution)/shard_map/ppermute | solution.py:201
  13.4 30.8 %collective-permute-start.9 = (bf16[33,16,256]{2,1,0:T(8,128)(2,1)}, bf16[33,16,256]{2,1,0:T(8,128)(2,1)S(1)}, u32[]{:S(2)}, u32[]{:S(2)}) collective-permute-start(bf16[33,16,256]{2,1,0:T(8,128)(2,1)} %get-tuple-element.32), channel_id=1, source_target_pairs={{0,31},{1,30},{2,1},{3,0},{4,3},{5,2},{6,5},{7,4},{8,7},{9,6},{10,... | collective-permute-start | bytes 811016 | tf_op jit(solution)/shard_map/ppermute | solution.py:201
  19.3 37.6 %copy-start.7 = (bf16[32,16,256]{2,1,0:T(8,128)(2,1)}, bf16[32,16,256]{2,1,0:T(8,128)(2,1)S(1)}, u32[]{:S(2)}) copy-start(bf16[32,16,256]{2,1,0:T(8,128)(2,1)S(1)} %collective-permute-done.4.refs_1_) | copy-start | bytes 786436
  19.3 37.6 %collective-permute-start.5 = (bf16[33,16,256]{2,1,0:T(8,128)(2,1)}, bf16[33,16,256]{2,1,0:T(8,128)(2,1)S(1)}, u32[]{:S(2)}, u32[]{:S(2)}) collective-permute-start(bf16[33,16,256]{2,1,0:T(8,128)(2,1)} %get-tuple-element.27), channel_id=1, source_target_pairs={{0,28},{1,29},{2,30},{3,31},{4,0},{5,1},{6,2},{7,3},{8,4},{9,5},{1... | collective-permute-start | bytes 811016 | tf_op jit(solution)/shard_map/ppermute | solution.py:201
  25.0 25.3 %copy-start.8 = (bf16[32,16,256]{2,1,0:T(8,128)(2,1)}, bf16[32,16,256]{2,1,0:T(8,128)(2,1)S(1)}, u32[]{:S(2)}) copy-start(bf16[32,16,256]{2,1,0:T(8,128)(2,1)S(1)} %collective-permute-done.7.refs_1_) | copy-start | bytes 786436
  25.0 32.0 %collective-permute-start.6 = (bf16[33,16,256]{2,1,0:T(8,128)(2,1)}, bf16[33,16,256]{2,1,0:T(8,128)(2,1)S(1)}, u32[]{:S(2)}, u32[]{:S(2)}) collective-permute-start(bf16[33,16,256]{2,1,0:T(8,128)(2,1)} %get-tuple-element.28), channel_id=1, source_target_pairs={{0,29},{1,28},{2,31},{3,30},{4,1},{5,0},{6,3},{7,2},{8,5},{9,4},{1... | collective-permute-start | bytes 811016 | tf_op jit(solution)/shard_map/ppermute | solution.py:201
  30.8 14.0 %copy-start = (bf16[33,16,256]{2,1,0:T(8,128)(2,1)}, bf16[33,16,256]{2,1,0:T(8,128)(2,1)S(1)}, u32[]{:S(2)}) copy-start(bf16[33,16,256]{2,1,0:T(8,128)(2,1)S(1)} %collective-permute-done.3.refs_1_.refs_3_.refs_5_.refs_7_) | copy-start | bytes 811012
  30.8 33.6 %collective-permute-start.1 = (bf16[33,16,256]{2,1,0:T(8,128)(2,1)}, bf16[33,16,256]{2,1,0:T(8,128)(2,1)S(1)}, u32[]{:S(2)}, u32[]{:S(2)}) collective-permute-start(bf16[33,16,256]{2,1,0:T(8,128)(2,1)} %get-tuple-element.21), channel_id=1, source_target_pairs={{0,26},{1,27},{2,28},{3,29},{4,30},{5,31},{6,0},{7,1},{8,2},{9,3},... | collective-permute-start | bytes 811016 | tf_op jit(solution)/shard_map/ppermute | solution.py:201
  31.8 18.6 %copy-start.3 = (bf16[33,16,256]{2,1,0:T(8,128)(2,1)}, bf16[33,16,256]{2,1,0:T(8,128)(2,1)S(1)}, u32[]{:S(2)}) copy-start(bf16[33,16,256]{2,1,0:T(8,128)(2,1)S(1)} %collective-permute-done.8.refs_2_.refs_6_) | copy-start | bytes 811012
  31.8 32.6 %collective-permute-start.2 = (bf16[33,16,256]{2,1,0:T(8,128)(2,1)}, bf16[33,16,256]{2,1,0:T(8,128)(2,1)S(1)}, u32[]{:S(2)}, u32[]{:S(2)}) collective-permute-start(bf16[33,16,256]{2,1,0:T(8,128)(2,1)} %get-tuple-element.22), channel_id=1, source_target_pairs={{0,27},{1,26},{2,29},{3,28},{4,31},{5,30},{6,1},{7,0},{8,3},{9,2},... | collective-permute-start | bytes 811016 | tf_op jit(solution)/shard_map/ppermute | solution.py:201
  44.2 6.1 %copy-start.5 = (bf16[33,16,256]{2,1,0:T(8,128)(2,1)}, bf16[33,16,256]{2,1,0:T(8,128)(2,1)S(1)}, u32[]{:S(2)}) copy-start(bf16[33,16,256]{2,1,0:T(8,128)(2,1)S(1)} %collective-permute-done.9.refs_3_.refs_7_) | copy-start | bytes 811012
  44.2 20.1 %collective-permute-start = (bf16[32,16,256]{2,1,0:T(8,128)(2,1)}, bf16[32,16,256]{2,1,0:T(8,128)(2,1)S(1)}, u32[]{:S(2)}, u32[]{:S(2)}) collective-permute-start(bf16[32,16,256]{2,1,0:T(8,128)(2,1)} %get-tuple-element.20), channel_id=1, source_target_pairs={{0,1},{1,0},{2,3},{3,2},{4,5},{5,4},{6,7},{7,6},{8,9},{9,8},{10,11... | collective-permute-start | bytes 786440 | tf_op jit(solution)/shard_map/ppermute | solution.py:201
  56.9 0.7 %copy-start.2 = (bf16[33,16,256]{2,1,0:T(8,128)(2,1)}, bf16[33,16,256]{2,1,0:T(8,128)(2,1)S(1)}, u32[]{:S(2)}) copy-start(bf16[33,16,256]{2,1,0:T(8,128)(2,1)S(1)} %collective-permute-done.5.refs_2_.refs_6_) | copy-start | bytes 811012
  57.0 0.8 %copy-start.6 = (bf16[33,16,256]{2,1,0:T(8,128)(2,1)}, bf16[33,16,256]{2,1,0:T(8,128)(2,1)S(1)}, u32[]{:S(2)}) copy-start(bf16[33,16,256]{2,1,0:T(8,128)(2,1)S(1)} %collective-permute-done.6.refs_3_.refs_7_) | copy-start | bytes 811012
  64.3 0.7 copy-start.9
  64.4 0.8 %copy-start.1 = (bf16[33,16,256]{2,1,0:T(8,128)(2,1)}, bf16[33,16,256]{2,1,0:T(8,128)(2,1)S(1)}, u32[]{:S(2)}) copy-start(bf16[33,16,256]{2,1,0:T(8,128)(2,1)S(1)} %collective-permute-done.1.refs_2_.refs_6_) | copy-start | bytes 811012
  64.4 0.8 %copy-start.4 = (bf16[33,16,256]{2,1,0:T(8,128)(2,1)}, bf16[33,16,256]{2,1,0:T(8,128)(2,1)S(1)}, u32[]{:S(2)}) copy-start(bf16[33,16,256]{2,1,0:T(8,128)(2,1)S(1)} %collective-permute-done.2.refs_3_.refs_7_) | copy-start | bytes 811012

commit v2 on v1

v2 whole, which is shorter than its diff:
```python
import functools

import jax
import jax.numpy as jnp
import ml_dtypes
import numpy as np
from jax import lax
from jax.experimental import pallas as pl
from jax.experimental.pallas import tpu as pltpu
from jax.sharding import PartitionSpec as P

NB = 256
BW = 64
PAIRS = 4
LANES = 128
LIFT = 1024.0
CROSS_VMEM = 20 << 20


def dft_table(nbins, length):
    freq = np.arange(nbins)[:, None]
    sample = np.arange(length)[None, :]
    phase = (freq * sample % length) * (2.0 * np.pi / length)
    window = 0.5 - 0.5 * np.cos(sample * (2.0 * np.pi / length))
    table = np.concatenate([window * np.cos(phase), -window * np.sin(phase)])
    return (table.astype(np.float32).astype(ml_dtypes.bfloat16).astype(np.float32) * LIFT).astype(ml_dtypes.bfloat16)


def message_plan(seg):
    away = range(1, seg)
    plan = [((0, 1), False, k, True) for k in away]
    plan += [((1,), True, k, True) for k in away]
    plan += [((pair,), True, 0, True) for pair in range(1, PAIRS)]
    plan += [((2, 3), False, k, False) for k in away]
    plan += [((pair,), True, k, True) for pair in (2, 3) for k in away]
    return plan + [(tuple(range(PAIRS)), False, 0, True)]


def waits_for(message, seg):
    pairs, lent, shift, _ = message
    own = ((0, 1), False, shift, True)
    near = [((pair,), True, 0, True) for pair in range(1, PAIRS)]
    across = ((1,), True, shift, True)
    if pairs == (2, 3):
        return [own, *near[:2]]
    if pairs == (2,) and lent and shift:
        return [across]
    if pairs == (3,) and lent and shift:
        return [across]
    return []


def split3(x):
    high = x.astype(jnp.bfloat16)
    rest = x - high.astype(jnp.float32)
    mid = rest.astype(jnp.bfloat16)
    low = (rest - mid.astype(jnp.float32)).astype(jnp.bfloat16)
    return high, mid, low


def first_bin(band_ref, pair, lent, shift, seg):
    block, seat, chan = lax.axis_index("chan"), lax.axis_index("seg"), band_ref.shape[1]
    user = lax.rem(block + (chan - pair), chan) if lent else block
    return band_ref[pair, user] + lax.rem(seat + shift, seg) * (BW // seg)


def spectra_kernel(plan, seg, band_ref, table_hbm, signal_hbm, *refs):
    n = len(plan)
    outs, (table, signal, raw, spectra, table_sem, signal_sem, out_sem) = refs[:n], refs[n:]
    segs, _, width = signal.shape
    nbins = table.shape[0] // 2
    rows = 2 * segs
    bins = BW // seg
    table_copy = pltpu.make_async_copy(table_hbm, table, table_sem)
    signal_copy = pltpu.make_async_copy(signal_hbm, signal, signal_sem)
    table_copy.start()
    signal_copy.start()
    table_copy.wait()
    signal_copy.wait()
    power = jnp.zeros((8, width), jnp.float32)
    for s in range(segs):
        spectrum = jnp.dot(table[...], signal[s], preferred_element_type=jnp.float32)
        for r in range(2):
            for h in range(width // LANES):
                raw[h, pl.ds(r * segs + s, nbins, stride=rows), :] = spectrum[r * nbins : (r + 1) * nbins, h * LANES : (h + 1) * LANES]
        x = signal[s].astype(jnp.float32)
        power = power + jnp.sum((x * x).reshape(-1, 8, width), axis=0)
    parts = split3(jnp.sum(power, axis=0, keepdims=True))
    row = lax.broadcasted_iota(jnp.int32, (rows, width), 0)
    packed = jnp.zeros((rows, width), jnp.float32)
    for i, part in enumerate(parts):
        packed = jnp.where(row == i, part.astype(jnp.float32), packed)
    spectra[nbins] = packed.astype(jnp.bfloat16)
    for h in range(width // LANES):
        spectra[:nbins, :, h * LANES : (h + 1) * LANES] = raw[h].reshape(nbins, rows, LANES).astype(jnp.bfloat16)
    copies = []
    for (pairs, lent, shift, powered), out in zip(plan, outs):
        pieces = [(first_bin(band_ref, pair, lent, shift, seg), bins) for pair in pairs] + [(nbins, 1)] * powered
        for i, (start, size) in enumerate(pieces):
            copies.append(pltpu.make_async_copy(spectra.at[pl.ds(start, size)], out.at[pl.ds(i * bins, size)], out_sem.at[len(copies)]))
    for copy in copies:
        copy.start()
    for copy in copies:
        copy.wait()


def message_shape(message, bins, rows, width):
    pairs, _, _, powered = message
    return jax.ShapeDtypeStruct((len(pairs) * bins + powered, rows, width), jnp.bfloat16)


def make_spectra(plan, seg, band, table, signal):
    segs, length, width = signal.shape
    rows, bins, n, nbins = 2 * segs, BW // seg, len(plan), table.shape[0] // 2
    anywhere = pl.BlockSpec(memory_space=pl.ANY)
    return pl.pallas_call(
        functools.partial(spectra_kernel, plan, seg),
        in_specs=[pl.BlockSpec(memory_space=pltpu.SMEM), anywhere, anywhere],
        out_specs=[anywhere] * n,
        out_shape=[message_shape(m, bins, rows, width) for m in plan],
        scratch_shapes=[
            pltpu.VMEM(table.shape, jnp.bfloat16),
            pltpu.VMEM(signal.shape, jnp.bfloat16),
            pltpu.VMEM((width // LANES, nbins * rows, LANES), jnp.float32),
            pltpu.VMEM((nbins + 1, rows, width), jnp.bfloat16),
            pltpu.SemaphoreType.DMA,
            pltpu.SemaphoreType.DMA,
            pltpu.SemaphoreType.DMA((sum(len(m[0]) + m[3] for m in plan),)),
        ],
        compiler_params=pltpu.CompilerParams(vmem_limit_bytes=56 << 20),
    )(band, table, signal)


def turned(y):
    half = y.shape[0] // 2
    return jnp.concatenate([-y[half:], y[:half]], axis=0)


def inv_rms_of(tiles, samples):
    power = 0.0
    for tile in tiles:
        t = tile.astype(jnp.float32)
        power = power + (t[0:1] + t[1:2] + t[2:3])
    return lax.rsqrt(power / samples + 1e-06)


def cross_kernel(pair, firsts, samples, scale, sched_ref, *refs):
    n = len(firsts)
    arrays, (out, held, ring, weight, in_sem, out_sem) = refs[:n], refs[-6:]
    _, bins, _, width = held.shape
    depth, _, chunk = ring.shape[:3]
    steps = bins // chunk
    out_copies = [
        pltpu.make_async_copy(ring.at[c % depth], out.at[0, pair, :, pl.ds(c * chunk, chunk)], out_sem.at[c]) for c in range(steps)
    ]
    zero_copies = [pltpu.make_async_copy(ring.at[0], out.at[0, pair, :, pl.ds(c * chunk, chunk)], out_sem.at[c]) for c in range(steps)]
    live = sched_ref[0, pair]

    @pl.when(live == 0)
    def _():
        ring[0] = jnp.zeros(ring.shape[1:], ring.dtype)
        for copy in zero_copies:
            copy.start()
        for copy in zero_copies:
            copy.wait()

    @pl.when(live != 0)
    def _():
        copies = [
            pltpu.make_async_copy(array.at[pl.ds(first, size)], held.at[k, pl.ds(0, size)], in_sem.at[k])
            for k, (array, (first, size)) in enumerate(zip(arrays, firsts))
        ]
        for copy in copies:
            copy.start()
        for copy in copies:
            copy.wait()
        tiles = [k for k in range(n) if firsts[k][1] == 1]
        blocks = [k for k in range(n) if firsts[k][1] != 1]
        halves = 2 if pair else 1
        mine, theirs = blocks[: len(blocks) // halves], blocks[-(len(blocks) // halves) :]
        my_power, their_power = tiles[: len(tiles) // halves], tiles[-(len(tiles) // halves) :]
        by_row = jnp.broadcast_to(inv_rms_of([held[k, 0] for k in my_power], samples) * scale, (width, width)).T
        weight[...] = by_row * inv_rms_of([held[k, 0] for k in their_power], samples)
        for c in range(steps):
            if c >= depth:
                out_copies[c - depth].wait()
            for f in range(c * chunk, (c + 1) * chunk):
                x = jnp.concatenate([held[k, f] for k in mine], axis=0)
                y = jnp.concatenate([held[k, f] for k in theirs], axis=0)
                y_turned = jnp.concatenate([turned(held[k, f]) for k in theirs], axis=0)
                partner = jnp.concatenate([y, y_turned], axis=1)
                product = lax.dot_general(x, partner, (((0,), (0,)), ((), ())), preferred_element_type=jnp.float32)
                for r in range(2):
                    part = product[:, r * width : (r + 1) * width] * weight[...]
                    ring[c % depth, r, f - c * chunk] = part.astype(ring.dtype)
            out_copies[c].start()
        for c in range(max(steps - depth, 0), steps):
            out_copies[c].wait()


def cross(pair, samples, scale, sched, mine, theirs, my_power, their_power, shape, out):
    rows, width = mine[0][0].shape[1:]
    bins = shape[3]
    chunk = min(4, bins)
    blocks = mine + theirs if pair else mine
    tiles = my_power + their_power if pair else my_power
    arrays = [array for array, _ in blocks] + tiles
    firsts = [(first, bins) for _, first in blocks] + [(array.shape[0] - 1, 1) for array in tiles]
    anywhere = pl.BlockSpec(memory_space=pl.ANY)
    operands = [sched, *arrays]
    aliases = {}
    if out is not None:
        aliases = {len(operands): 0}
        operands.append(out)
    return pl.pallas_call(
        functools.partial(cross_kernel, pair, firsts, samples, scale),
        in_specs=[pl.BlockSpec(memory_space=pltpu.SMEM)] + [anywhere] * (len(operands) - 1),
        out_specs=anywhere,
        scratch_shapes=[
            pltpu.VMEM((len(firsts), bins, rows, width), jnp.bfloat16),
            pltpu.VMEM((4, 2, chunk, width, width), jnp.bfloat16),
            pltpu.VMEM((width, width), jnp.float32),
            pltpu.SemaphoreType.DMA((len(firsts),)),
            pltpu.SemaphoreType.DMA((bins // chunk,)),
        ],
        out_shape=jax.ShapeDtypeStruct(shape, jnp.bfloat16),
        input_output_aliases=aliases,
        compiler_params=pltpu.CompilerParams(vmem_limit_bytes=CROSS_VMEM),
        cost_estimate=pl.CostEstimate(
            flops=4 * bins * len(mine) * rows * width * width, bytes_accessed=4 * bins * width * width, transcendentals=0
        ),
    )(*operands)


def body(signal, band, sched):
    seg_dev, length, width = signal.shape
    seg, chan = lax.axis_size("seg"), lax.axis_size("chan")
    segs = seg_dev * seg
    bins = BW // seg
    plan = message_plan(seg)
    table = jnp.asarray(dft_table(NB, length))
    cuts = make_spectra(plan, seg, band.T, table, signal)

    def delivered(message, cut):
        pairs, lent, shift, _ = message
        away = pairs[0] if lent else 0
        if not away and not shift:
            return cut
        route = [(c * seg + s, (c - away) % chan * seg + (s + shift) % seg) for c in range(chan) for s in range(seg)]
        return lax.ppermute(cut, ("chan", "seg"), route)

    windows, powers, done = {}, {}, {}
    for message, cut in zip(plan, cuts):
        pairs, lent, shift, powered = message
        earlier = [done[m] for m in waits_for(message, seg)]
        if earlier:
            cut, *_ = lax.optimization_barrier((cut, *earlier))
        array = done[message] = delivered(message, cut)
        for i, pair in enumerate(pairs):
            windows[pair, lent, shift] = array, i * bins
            if powered:
                powers[pair, lent, shift] = array
    scale = 1.0 / (segs * 0.375 * length) / LIFT**2
    shape = (1, PAIRS, 2, bins, width, width)
    my_power = [powers[0, False, k] for k in range(seg)]
    out = None
    for pair in range(PAIRS):
        mine = [windows[pair, False, k] for k in range(seg)]
        theirs = [windows[pair, True, k] for k in range(seg)] if pair else mine
        their_power = [powers[pair, True, k] for k in range(seg)] if pair else my_power
        out = cross(pair, segs * length, scale, sched, mine, theirs, my_power, their_power, shape, out)
    return out


def solution(mesh):
    in_specs = (P("seg", None, "chan"), P(), P("chan", None))
    out_specs = P("chan", None, None, "seg", None, None)
    return jax.shard_map(body, mesh=mesh, in_specs=in_specs, out_specs=out_specs, check_vma=False)
```

time: 71.8 us -> 62.6 us (0.87)
  the two profiles are of different devices: /device:TPU:4 before, /device:TPU:0 now
where the time goes in v2:
time: 62.6 us; the launch traced here: 61.5 us
  Pallas kernels  26 us (42%)
  waiting for transfers between devices  17.1 us (27%)
  starting transfers between devices  16.3 us (26%)
  local copies, waits for them, and re-layouts  1.88 us (3%)
    pallas_call x4, Pallas kernels, cross(): pl.pallas_call(functools.partial(cross_kernel, pair, firsts, samples, sca...  17.2 us
    ppermute x8, waiting for transfers between devices, delivered(): return lax.ppermute(cut, ('chan', 'seg'), route)  17.1 us
    ppermute x8, starting transfers between devices, delivered(): return lax.ppermute(cut, ('chan', 'seg'), route)  16.3 us
    pallas_call x1, Pallas kernels, make_spectra(): pl.pallas_call(functools.partial(spectra_kernel, plan, seg), in_specs=[pl...  8.74 us
    unnamed x4, local copies, waits for them, and re-layouts  1.88 us
  transfers between devices with their start and end apart: 8, of which 4 were waited for; matrix products, arithmetic and copies ran while one was open for 0% of the time, Pallas kernels for 21%

profile of v2, /device:TPU:0, one launch (start us, length us, event | category | flops | bytes accessed | tf_op | source)
XLA Modules:
  0.0 61.5 jit_solution(14261092884387835777)
XLA Ops:
  0.0 8.7 %shard_map.46 = (bf16[65,16,256]{2,1,0:T(8,128)(2,1)}, bf16[33,16,256]{2,1,0:T(8,128)(2,1)}, bf16[33,16,256]{2,1,0:T(8,128)(2,1)}, bf16[33,16,256]{2,1,0:T(8,128...) custom-call(s32[4,16]{1,0:T(4,128)} %bitcast.1, ...), custom_call_target="tpu_custom_call" | custom-call | tf_op jit(solution)/shard_map/pallas_call | solution.py:116
  8.8 3.0 %collective-permute-start = (bf16[65,16,256]{2,1,0:T(8,128)(2,1)}, bf16[65,16,256]{2,1,0:T(8,128)(2,1)S(1)}, u32[]{:S(2)}, u32[]{:S(2)}) collective-permute-start(bf16[65,16,256]{2,1,0:T(8,128)(2,1)} %get-tuple-element.19), channel_id=1, source_target_pairs={{0,1},{1,0},{2,3},{3,2},{4,5},{5,4},{6,7},{7,6},{8,9},{9,8},{10,11... | collective-permute-start | bytes 1597448 | tf_op jit(solution)/shard_map/ppermute | solution.py:250
  11.8 3.7 %collective-permute-start.1 = (bf16[33,16,256]{2,1,0:T(8,128)(2,1)}, bf16[33,16,256]{2,1,0:T(8,128)(2,1)S(1)}, u32[]{:S(2)}, u32[]{:S(2)}) collective-permute-start(bf16[33,16,256]{2,1,0:T(8,128)(2,1)} %get-tuple-element.20), channel_id=1, source_target_pairs={{0,30},{1,31},{2,0},{3,1},{4,2},{5,3},{6,4},{7,5},{8,6},{9,7},{10,... | collective-permute-start | bytes 811016 | tf_op jit(solution)/shard_map/ppermute | solution.py:250
  15.5 0.8 %collective-permute-start.2 = (bf16[33,16,256]{2,1,0:T(8,128)(2,1)}, bf16[33,16,256]{2,1,0:T(8,128)(2,1)S(1)}, u32[]{:S(2)}, u32[]{:S(2)}) collective-permute-start(bf16[33,16,256]{2,1,0:T(8,128)(2,1)} %get-tuple-element.21), channel_id=1, source_target_pairs={{0,28},{1,29},{2,30},{3,31},{4,0},{5,1},{6,2},{7,3},{8,4},{9,5},{1... | collective-permute-start | bytes 811016 | tf_op jit(solution)/shard_map/ppermute | solution.py:250
  16.3 0.3 collective-permute-start.5
  16.6 5.7 %collective-permute-done.1.refs_2_.refs_6_ = bf16[33,16,256]{2,1,0:T(8,128)(2,1)S(1)} collective-permute-done((bf16[33,16,256]{2,1,0:T(8,128)(2,1)}, bf16[33,16,256]{2,1,0:T(8,128)(2,1)S(1)}, u32[]{:S(2)}, u32[]{:S(2)}) %collective-permute-start.1) | collective-permute-done | bytes 270368 | tf_op jit(solution)/shard_map/ppermute | solution.py:250
  22.4 3.2 %collective-permute-done.2.refs_2_.refs_6_ = bf16[33,16,256]{2,1,0:T(8,128)(2,1)S(1)} collective-permute-done((bf16[33,16,256]{2,1,0:T(8,128)(2,1)}, bf16[33,16,256]{2,1,0:T(8,128)(2,1)S(1)}, u32[]{:S(2)}, u32[]{:S(2)}) %collective-permute-start.2) | collective-permute-done | bytes 270368 | tf_op jit(solution)/shard_map/ppermute | solution.py:250
  25.6 2.2 %collective-permute-done.refs_1_.refs_3_.refs_5_ = bf16[65,16,256]{2,1,0:T(8,128)(2,1)S(1)} collective-permute-done((bf16[65,16,256]{2,1,0:T(8,128)(2,1)}, bf16[65,16,256]{2,1,0:T(8,128)(2,1)S(1)}, u32[]{:S(2)}, u32[]{:S(2)}) %collective-permute-start) | collective-permute-done | bytes 532512 | tf_op jit(solution)/shard_map/ppermute | solution.py:250
  27.8 2.1 %collective-permute-start.3 = (bf16[64,16,256]{2,1,0:T(8,128)(2,1)}, bf16[64,16,256]{2,1,0:T(8,128)(2,1)S(1)}, u32[]{:S(2)}, u32[]{:S(2)}) collective-permute-start(bf16[64,16,256]{2,1,0:T(8,128)(2,1)} %get-tuple-element.22), channel_id=1, source_target_pairs={{0,1},{1,0},{2,3},{3,2},{4,5},{5,4},{6,7},{7,6},{8,9},{9,8},{10,11... | collective-permute-start | bytes 1572872 | tf_op jit(solution)/shard_map/ppermute | solution.py:250
  29.9 0.0 collective-permute-done.5.refs_3_.refs_7_
  29.9 5.0 %collective-permute-start.7 = (bf16[33,16,256]{2,1,0:T(8,128)(2,1)}, bf16[33,16,256]{2,1,0:T(8,128)(2,1)S(1)}, u32[]{:S(2)}, u32[]{:S(2)}) collective-permute-start(bf16[33,16,256]{2,1,0:T(8,128)(2,1)} %get-tuple-element.28), channel_id=1, source_target_pairs={{0,29},{1,28},{2,31},{3,30},{4,1},{5,0},{6,3},{7,2},{8,5},{9,4},{1... | collective-permute-start | bytes 811016 | tf_op jit(solution)/shard_map/ppermute | solution.py:250
  34.9 0.3 collective-permute-start.4
  35.2 1.0 %collective-permute-start.6 = (bf16[33,16,256]{2,1,0:T(8,128)(2,1)}, bf16[33,16,256]{2,1,0:T(8,128)(2,1)S(1)}, u32[]{:S(2)}, u32[]{:S(2)}) collective-permute-start(bf16[33,16,256]{2,1,0:T(8,128)(2,1)} %get-tuple-element.26), channel_id=1, source_target_pairs={{0,27},{1,26},{2,29},{3,28},{4,31},{5,30},{6,1},{7,0},{8,3},{9,2},... | collective-permute-start | bytes 811016 | tf_op jit(solution)/shard_map/ppermute | solution.py:250
  36.2 0.0 copy-start
  36.2 1.2 %copy-done = bf16[129,16,256]{2,1,0:T(8,128)(2,1)S(1)} copy-done((bf16[129,16,256]{2,1,0:T(8,128)(2,1)S(1)}, bf16[129,16,256]{2,1,0:T(8,128)(2,1)}, u32[]{:S(2)}) %copy-start) | copy-done | bytes 1056792
  37.5 0.0 copy-start.1
  37.5 0.7 %copy-done.1 = s32[1,4]{1,0:T(1,128)S(1)} copy-done((s32[1,4]{1,0:T(1,128)S(1)}, s32[1,4]{1,0:T(1,128)}, u32[]{:S(2)}) %copy-start.1) | copy-done | bytes 40
  38.1 4.0 %shard_map.47.refs_8_ = bf16[1,4,2,32,256,256]{5,4,3,2,1,0:T(8,128)(2,1)} custom-call(s32[1,4]{1,0:T(1,128)S(1)} %copy-done.1, bf16[129,16,256]{2,1,0:T(8,128)(2,1)S(1)} %copy-done, bf16[65,16,256]{2,1,0:T(8,128)(2,1)S(1)} %collective-permute-done.refs_1_.refs_3_.refs_5_, bf16[129,16,256]{2,1,0:T(8,128)(2,1)S(1)} %copy-done, ...), custom_call_target="tpu_custom_call" | custom-call | flops 268435456 | bytes 8388608 | tf_op jit(solution)/shard_map/pallas_call | solution.py:215
  42.1 4.1 %shard_map.48.refs_8_ = bf16[1,4,2,32,256,256]{5,4,3,2,1,0:T(8,128)(2,1)} custom-call(s32[1,4]{1,0:T(1,128)S(1)} %copy-done.1, bf16[129,16,256]{2,1,0:T(8,128)(2,1)S(1)} %copy-done, bf16[65,16,256]{2,1,0:T(8,128)(2,1)S(1)} %collective-permute-done.refs_1_.refs_3_.refs_5_, ...), custom_call_target="tpu_custom_call", output_to_operand_aliasing={{}: (9, {})} | custom-call | flops 268435456 | bytes 8388608 | tf_op jit(solution)/shard_map/pallas_call | solution.py:215
  46.2 5.9 %collective-permute-done.7.refs_3_.refs_7_ = bf16[33,16,256]{2,1,0:T(8,128)(2,1)S(1)} collective-permute-done((bf16[33,16,256]{2,1,0:T(8,128)(2,1)}, bf16[33,16,256]{2,1,0:T(8,128)(2,1)S(1)}, u32[]{:S(2)}, u32[]{:S(2)}) %collective-permute-start.7) | collective-permute-done | bytes 270368 | tf_op jit(solution)/shard_map/ppermute | solution.py:250
  52.1 0.0 collective-permute-done.3.refs_1_
  52.1 5.1 %shard_map.49.refs_8_ = bf16[1,4,2,32,256,256]{5,4,3,2,1,0:T(8,128)(2,1)} custom-call(s32[1,4]{1,0:T(1,128)S(1)} %copy-done.1, bf16[129,16,256]{2,1,0:T(8,128)(2,1)S(1)} %copy-done, bf16[64,16,256]{2,1,0:T(8,128)(2,1)S(1)} %collective-permute-done.3.refs_1_, ...), custom_call_target="tpu_custom_call", output_to_operand_aliasing={{}: (9, {})} | custom-call | flops 268435456 | bytes 8388608 | tf_op jit(solution)/shard_map/pallas_call | solution.py:215
  57.3 0.0 collective-permute-done.4.refs_2_.refs_6_
  57.3 0.0 collective-permute-done.6.refs_3_.refs_7_
  57.3 4.1 %shard_map.50 = bf16[1,4,2,32,256,256]{5,4,3,2,1,0:T(8,128)(2,1)} custom-call(s32[1,4]{1,0:T(1,128)S(1)} %copy-done.1, bf16[129,16,256]{2,1,0:T(8,128)(2,1)S(1)} %copy-done, bf16[64,16,256]{2,1,0:T(8,128)(2,1)S(1)} %collective-permute-done.3.refs_1_, bf16[33,16,256]{2,1,0:T(8,128)(2,1)S(1)} %collective-permute-done.4.refs_2_.refs_6_, ...), custom_call_target="tpu_custom_call", output_to_operand_aliasing={{}: (9, {})} | custom-call | flops 268435456 | bytes 8388608 | tf_op jit(solution)/shard_map/pallas_call | solution.py:215
Async XLA Ops:
  8.8 19.0 %collective-permute-start = (bf16[65,16,256]{2,1,0:T(8,128)(2,1)}, bf16[65,16,256]{2,1,0:T(8,128)(2,1)S(1)}, u32[]{:S(2)}, u32[]{:S(2)}) collective-permute-start(bf16[65,16,256]{2,1,0:T(8,128)(2,1)} %get-tuple-element.19), channel_id=1, source_target_pairs={{0,1},{1,0},{2,3},{3,2},{4,5},{5,4},{6,7},{7,6},{8,9},{9,8},{10,11... | collective-permute-start | bytes 1597448 | tf_op jit(solution)/shard_map/ppermute | solution.py:250
  11.8 10.6 %collective-permute-start.1 = (bf16[33,16,256]{2,1,0:T(8,128)(2,1)}, bf16[33,16,256]{2,1,0:T(8,128)(2,1)S(1)}, u32[]{:S(2)}, u32[]{:S(2)}) collective-permute-start(bf16[33,16,256]{2,1,0:T(8,128)(2,1)} %get-tuple-element.20), channel_id=1, source_target_pairs={{0,30},{1,31},{2,0},{3,1},{4,2},{5,3},{6,4},{7,5},{8,6},{9,7},{10,... | collective-permute-start | bytes 811016 | tf_op jit(solution)/shard_map/ppermute | solution.py:250
  15.5 10.1 %collective-permute-start.2 = (bf16[33,16,256]{2,1,0:T(8,128)(2,1)}, bf16[33,16,256]{2,1,0:T(8,128)(2,1)S(1)}, u32[]{:S(2)}, u32[]{:S(2)}) collective-permute-start(bf16[33,16,256]{2,1,0:T(8,128)(2,1)} %get-tuple-element.21), channel_id=1, source_target_pairs={{0,28},{1,29},{2,30},{3,31},{4,0},{5,1},{6,2},{7,3},{8,4},{9,5},{1... | collective-permute-start | bytes 811016 | tf_op jit(solution)/shard_map/ppermute | solution.py:250
  16.3 13.5 %collective-permute-start.5 = (bf16[33,16,256]{2,1,0:T(8,128)(2,1)}, bf16[33,16,256]{2,1,0:T(8,128)(2,1)S(1)}, u32[]{:S(2)}, u32[]{:S(2)}) collective-permute-start(bf16[33,16,256]{2,1,0:T(8,128)(2,1)} %get-tuple-element.25), channel_id=1, source_target_pairs={{0,31},{1,30},{2,1},{3,0},{4,3},{5,2},{6,5},{7,4},{8,7},{9,6},{10,... | collective-permute-start | bytes 811016 | tf_op jit(solution)/shard_map/ppermute | solution.py:250
  27.8 24.3 %collective-permute-start.3 = (bf16[64,16,256]{2,1,0:T(8,128)(2,1)}, bf16[64,16,256]{2,1,0:T(8,128)(2,1)S(1)}, u32[]{:S(2)}, u32[]{:S(2)}) collective-permute-start(bf16[64,16,256]{2,1,0:T(8,128)(2,1)} %get-tuple-element.22), channel_id=1, source_target_pairs={{0,1},{1,0},{2,3},{3,2},{4,5},{5,4},{6,7},{7,6},{8,9},{9,8},{10,11... | collective-permute-start | bytes 1572872 | tf_op jit(solution)/shard_map/ppermute | solution.py:250
  29.9 22.3 %collective-permute-start.7 = (bf16[33,16,256]{2,1,0:T(8,128)(2,1)}, bf16[33,16,256]{2,1,0:T(8,128)(2,1)S(1)}, u32[]{:S(2)}, u32[]{:S(2)}) collective-permute-start(bf16[33,16,256]{2,1,0:T(8,128)(2,1)} %get-tuple-element.28), channel_id=1, source_target_pairs={{0,29},{1,28},{2,31},{3,30},{4,1},{5,0},{6,3},{7,2},{8,5},{9,4},{1... | collective-permute-start | bytes 811016 | tf_op jit(solution)/shard_map/ppermute | solution.py:250
  34.9 22.4 %collective-permute-start.4 = (bf16[33,16,256]{2,1,0:T(8,128)(2,1)}, bf16[33,16,256]{2,1,0:T(8,128)(2,1)S(1)}, u32[]{:S(2)}, u32[]{:S(2)}) collective-permute-start(bf16[33,16,256]{2,1,0:T(8,128)(2,1)} %get-tuple-element.23), channel_id=1, source_target_pairs={{0,26},{1,27},{2,28},{3,29},{4,30},{5,31},{6,0},{7,1},{8,2},{9,3},... | collective-permute-start | bytes 811016 | tf_op jit(solution)/shard_map/ppermute | solution.py:250
  35.2 22.0 %collective-permute-start.6 = (bf16[33,16,256]{2,1,0:T(8,128)(2,1)}, bf16[33,16,256]{2,1,0:T(8,128)(2,1)S(1)}, u32[]{:S(2)}, u32[]{:S(2)}) collective-permute-start(bf16[33,16,256]{2,1,0:T(8,128)(2,1)} %get-tuple-element.26), channel_id=1, source_target_pairs={{0,27},{1,26},{2,29},{3,28},{4,31},{5,30},{6,1},{7,0},{8,3},{9,2},... | collective-permute-start | bytes 811016 | tf_op jit(solution)/shard_map/ppermute | solution.py:250
  36.2 1.2 %copy-start = (bf16[129,16,256]{2,1,0:T(8,128)(2,1)S(1)}, bf16[129,16,256]{2,1,0:T(8,128)(2,1)}, u32[]{:S(2)}) copy-start(bf16[129,16,256]{2,1,0:T(8,128)(2,1)} %get-tuple-element.17.refs_0_.refs_2_.refs_4_) | copy-start | bytes 3170308
  37.5 0.7 %copy-start.1 = (s32[1,4]{1,0:T(1,128)S(1)}, s32[1,4]{1,0:T(1,128)}, u32[]{:S(2)}) copy-start(s32[1,4]{1,0:T(1,128)} %sched_ref.7) | copy-start | bytes 52

commit v3 on v2

v3 whole, which is shorter than its diff:
```python
import functools

import jax
import jax.numpy as jnp
import ml_dtypes
import numpy as np
from jax import lax
from jax.experimental import pallas as pl
from jax.experimental.pallas import tpu as pltpu
from jax.sharding import PartitionSpec as P

NB = 256
BW = 64
PAIRS = 4
LANES = 128
LIFT = 1024.0
CROSS_VMEM = 24 << 20
GROUPS = ((0,), (1,), (2, 3))


def dft_table(nbins, length):
    freq = np.arange(nbins)[:, None]
    sample = np.arange(length)[None, :]
    phase = (freq * sample % length) * (2.0 * np.pi / length)
    window = 0.5 - 0.5 * np.cos(sample * (2.0 * np.pi / length))
    table = np.concatenate([window * np.cos(phase), -window * np.sin(phase)])
    return (table.astype(np.float32).astype(ml_dtypes.bfloat16).astype(np.float32) * LIFT).astype(ml_dtypes.bfloat16)


def row_table(table):
    nbins, length = table.shape[0] // 2, table.shape[1]
    rows = table.astype(np.float32).reshape(2, nbins, length // LANES, LANES).transpose(0, 2, 1, 3)
    return np.pad(rows, ((0, 0), (0, 0), (0, 8), (0, 0)))


def message_plan(seg):
    away = range(1, seg)
    first = [((0, 1), False, k, True) for k in away]
    first += [((1,), True, k, True) for k in away]
    plan = [((pair,), True, 0, True) for pair in range(1, PAIRS)]
    plan += [((2, 3), False, k, False) for k in away]
    plan += [((pair,), True, k, True) for pair in (2, 3) for k in away]
    return first, plan + [(tuple(range(PAIRS)), False, 0, True)]


def comes_after(message):
    pairs, lent, shift, _ = message
    return 0 if lent and shift and pairs[0] > 1 else None


def split3(x):
    high = x.astype(jnp.bfloat16)
    rest = x - high.astype(jnp.float32)
    mid = rest.astype(jnp.bfloat16)
    low = (rest - mid.astype(jnp.float32)).astype(jnp.bfloat16)
    return high, mid, low


def first_bin(band_ref, pair, lent, shift, seg):
    block, seat, chan = lax.axis_index("chan"), lax.axis_index("seg"), band_ref.shape[1]
    user = lax.rem(block + (chan - pair), chan) if lent else block
    return band_ref[pair, user] + lax.rem(seat + shift, seg) * (BW // seg)


def power_tile(power, rows):
    width = power.shape[1]
    parts = split3(jnp.sum(power, axis=0, keepdims=True))
    row = lax.broadcasted_iota(jnp.int32, (rows, width), 0)
    packed = jnp.zeros((rows, width), jnp.float32)
    for i, part in enumerate(parts):
        packed = jnp.where(row == i, part.astype(jnp.float32), packed)
    return packed.astype(jnp.bfloat16)


def early_kernel(plan, seg, band_ref, rows_hbm, signal_hbm, *refs):
    n = len(plan)
    outs, (rows_held, signal, raw, cut, row_sem, signal_sem, out_sem) = refs[:n], refs[n:]
    segs, _, width = signal.shape
    rows, bins = 2 * segs, BW // seg
    windows = [first_bin(band_ref, pair, lent, shift, seg) for pairs, lent, shift, _ in plan for pair in pairs]
    row_copies = []
    for w, start in enumerate(windows):
        aligned = pl.multiple_of(start // 8 * 8, 8)
        row_copies.append(pltpu.make_async_copy(rows_hbm.at[:, :, pl.ds(aligned, bins + 8), :], rows_held.at[w], row_sem.at[w]))
    signal_copy = pltpu.make_async_copy(signal_hbm, signal, signal_sem)
    for copy in row_copies:
        copy.start()
    signal_copy.start()
    for copy in row_copies:
        copy.wait()
    pieces = []
    for w, start in enumerate(windows):
        for r in range(2):
            chunks = [rows_held[w, r, k, pl.ds(lax.rem(start, 8), bins), :] for k in range(rows_held.shape[2])]
            pieces.append(jnp.concatenate(chunks, axis=1))
    table = jnp.concatenate(pieces, axis=0).astype(jnp.bfloat16)
    signal_copy.wait()
    power = jnp.zeros((8, width), jnp.float32)
    for s in range(segs):
        spectrum = jnp.dot(table, signal[s], preferred_element_type=jnp.float32)
        for w in range(len(windows)):
            for r in range(2):
                at = (2 * w + r) * bins
                for h in range(width // LANES):
                    raw[h, pl.ds(w * bins * rows + r * segs + s, bins, stride=rows), :] = spectrum[at : at + bins, h * LANES : (h + 1) * LANES]
        x = signal[s].astype(jnp.float32)
        power = power + jnp.sum((x * x).reshape(-1, 8, width), axis=0)
    total = len(windows) * bins
    cut[total] = power_tile(power, rows)
    for h in range(width // LANES):
        cut[:total, :, h * LANES : (h + 1) * LANES] = raw[h].reshape(total, rows, LANES).astype(jnp.bfloat16)
    copies, at = [], 0
    for (pairs, _, _, _), out in zip(plan, outs):
        size = len(pairs) * bins
        copies.append(pltpu.make_async_copy(cut.at[pl.ds(at, size)], out.at[pl.ds(0, size)], out_sem.at[len(copies)]))
        copies.append(pltpu.make_async_copy(cut.at[pl.ds(total, 1)], out.at[pl.ds(size, 1)], out_sem.at[len(copies)]))
        at += size
    for copy in copies:
        copy.start()
    for copy in copies:
        copy.wait()


def early_spectra(plan, seg, band, rows_table, signal):
    segs, length, width = signal.shape
    rows, bins = 2 * segs, BW // seg
    n = sum(len(m[0]) for m in plan)
    anywhere = pl.BlockSpec(memory_space=pl.ANY)
    return pl.pallas_call(
        functools.partial(early_kernel, plan, seg),
        in_specs=[pl.BlockSpec(memory_space=pltpu.SMEM), anywhere, anywhere],
        out_specs=[anywhere] * len(plan),
        out_shape=[message_shape(m, bins, rows, width) for m in plan],
        scratch_shapes=[
            pltpu.VMEM((n, 2, length // LANES, bins + 8, LANES), jnp.float32),
            pltpu.VMEM(signal.shape, jnp.bfloat16),
            pltpu.VMEM((width // LANES, n * bins * rows, LANES), jnp.float32),
            pltpu.VMEM((n * bins + 1, rows, width), jnp.bfloat16),
            pltpu.SemaphoreType.DMA((n,)),
            pltpu.SemaphoreType.DMA,
            pltpu.SemaphoreType.DMA((2 * len(plan),)),
        ],
        compiler_params=pltpu.CompilerParams(vmem_limit_bytes=56 << 20),
    )(band, rows_table, signal)


def spectra_kernel(plan, seg, band_ref, table_hbm, signal_hbm, early_hbm, *refs):
    n = len(plan)
    outs, (table, signal, raw, spectra, table_sem, signal_sem, power_sem, out_sem) = refs[:n], refs[n:]
    segs, _, width = signal.shape
    nbins = table.shape[0] // 2
    rows = 2 * segs
    bins = BW // seg
    table_copy = pltpu.make_async_copy(table_hbm, table, table_sem)
    signal_copy = pltpu.make_async_copy(signal_hbm, signal, signal_sem)
    power_copy = pltpu.make_async_copy(early_hbm.at[pl.ds(early_hbm.shape[0] - 1, 1)], spectra.at[pl.ds(nbins, 1)], power_sem)
    table_copy.start()
    power_copy.start()
    signal_copy.start()
    table_copy.wait()
    power_copy.wait()
    signal_copy.wait()
    for s in range(segs):
        spectrum = jnp.dot(table[...], signal[s], preferred_element_type=jnp.float32)
        for r in range(2):
            for h in range(width // LANES):
                raw[h, pl.ds(r * segs + s, nbins, stride=rows), :] = spectrum[r * nbins : (r + 1) * nbins, h * LANES : (h + 1) * LANES]
    for h in range(width // LANES):
        spectra[:nbins, :, h * LANES : (h + 1) * LANES] = raw[h].reshape(nbins, rows, LANES).astype(jnp.bfloat16)
    copies = []
    for (pairs, lent, shift, powered), out in zip(plan, outs):
        pieces = [(first_bin(band_ref, pair, lent, shift, seg), bins) for pair in pairs] + [(nbins, 1)] * powered
        for i, (start, size) in enumerate(pieces):
            copies.append(pltpu.make_async_copy(spectra.at[pl.ds(start, size)], out.at[pl.ds(i * bins, size)], out_sem.at[len(copies)]))
    for copy in copies:
        copy.start()
    for copy in copies:
        copy.wait()


def message_shape(message, bins, rows, width):
    pairs, _, _, powered = message
    return jax.ShapeDtypeStruct((len(pairs) * bins + powered, rows, width), jnp.bfloat16)


def make_spectra(plan, seg, band, table, signal, early):
    segs, length, width = signal.shape
    rows, bins, n, nbins = 2 * segs, BW // seg, len(plan), table.shape[0] // 2
    anywhere = pl.BlockSpec(memory_space=pl.ANY)
    return pl.pallas_call(
        functools.partial(spectra_kernel, plan, seg),
        in_specs=[pl.BlockSpec(memory_space=pltpu.SMEM)] + [anywhere] * 3,
        out_specs=[anywhere] * n,
        out_shape=[message_shape(m, bins, rows, width) for m in plan],
        scratch_shapes=[
            pltpu.VMEM(table.shape, jnp.bfloat16),
            pltpu.VMEM(signal.shape, jnp.bfloat16),
            pltpu.VMEM((width // LANES, nbins * rows, LANES), jnp.float32),
            pltpu.VMEM((nbins + 1, rows, width), jnp.bfloat16),
            pltpu.SemaphoreType.DMA,
            pltpu.SemaphoreType.DMA,
            pltpu.SemaphoreType.DMA,
            pltpu.SemaphoreType.DMA((sum(len(m[0]) + m[3] for m in plan),)),
        ],
        compiler_params=pltpu.CompilerParams(vmem_limit_bytes=56 << 20),
        cost_estimate=pl.CostEstimate(flops=2 * table.size * segs * width, bytes_accessed=32 << 20, transcendentals=0),
    )(band, table, signal, early)


def turned(y):
    half = y.shape[0] // 2
    return jnp.concatenate([-y[half:], y[:half]], axis=0)


def inv_rms_of(tiles, samples):
    power = 0.0
    for tile in tiles:
        t = tile.astype(jnp.float32)
        power = power + (t[0:1] + t[1:2] + t[2:3])
    return lax.rsqrt(power / samples + 1e-06)


def cross_kernel(pairs, loads, samples, scale, sched_hbm, *refs):
    *arrays, out, sched_ref, held, ring, weight, sched_sem, in_sem, out_sem = refs
    sched_copy = pltpu.make_async_copy(sched_hbm, sched_ref, sched_sem)
    sched_copy.start()
    width = held.shape[-1]
    _, depth, _, chunk = ring.shape[:4]
    bins = out.shape[3]
    steps = bins // chunk
    in_copies, out_copies, zero_copies = {}, [], []
    for load in loads:
        for array, first, size, slot in sum(load, []):
            if slot not in in_copies:
                in_copies[slot] = pltpu.make_async_copy(arrays[array].at[pl.ds(first, size)], held.at[slot, pl.ds(0, size)], in_sem.at[slot])
    for i, pair in enumerate(pairs):
        for source, copies in ((lambda c: c % depth, out_copies), (lambda c: 0, zero_copies)):
            copies.append(
                [
                    pltpu.make_async_copy(ring.at[i, source(c)], out.at[0, pair, :, pl.ds(c * chunk, chunk)], out_sem.at[i, c])
                    for c in range(steps)
                ]
            )
    for copy in in_copies.values():
        copy.start()
    sched_copy.wait()
    waited = set()
    for i, pair in enumerate(pairs):
        x_loads, y_loads, x_power, y_power = ([slot for _, _, _, slot in part] for part in loads[i])
        for slot in x_loads + y_loads + x_power + y_power:
            if slot not in waited:
                in_copies[slot].wait()
                waited.add(slot)
        live = sched_ref[0, pair]

        @pl.when(live == 0)
        def _(i=i):
            ring[i, 0] = jnp.zeros(ring.shape[2:], ring.dtype)
            for c, copy in enumerate(zero_copies[i]):
                copy.start()
            for copy in zero_copies[i][: max(steps - depth, 0)]:
                copy.wait()

        @pl.when(live != 0)
        def _(i=i, x_loads=x_loads, y_loads=y_loads, x_power=x_power, y_power=y_power):
            by_row = jnp.broadcast_to(inv_rms_of([held[k, 0] for k in x_power], samples) * scale, (width, width)).T
            weight[...] = by_row * inv_rms_of([held[k, 0] for k in y_power], samples)
            for c in range(steps):
                if c >= depth:
                    out_copies[i][c - depth].wait()
                for f in range(c * chunk, (c + 1) * chunk):
                    x = jnp.concatenate([held[k, f] for k in x_loads], axis=0)
                    y = jnp.concatenate([held[k, f] for k in y_loads], axis=0)
                    y_turned = jnp.concatenate([turned(held[k, f]) for k in y_loads], axis=0)
                    partner = jnp.concatenate([y, y_turned], axis=1)
                    product = lax.dot_general(x, partner, (((0,), (0,)), ((), ())), preferred_element_type=jnp.float32)
                    for r in range(2):
                        part = product[:, r * width : (r + 1) * width] * weight[...]
                        ring[i, c % depth, r, f - c * chunk] = part.astype(ring.dtype)
                out_copies[i][c].start()

    for copies in out_copies:
        for copy in copies[max(steps - depth, 0) :]:
            copy.wait()


def cross(pairs, seg, samples, scale, sched, windows, powers, shape, out):
    bins, width = shape[3], shape[4]
    chunk = min(8, bins)
    arrays, slots, loads = [], {}, []

    def load(array, first, size):
        known = [k for k, other in enumerate(arrays) if other is array]
        if not known:
            arrays.append(array)
        where = (known[0] if known else len(arrays) - 1, first, size)
        return (*where, slots.setdefault(where, len(slots)))

    for pair in pairs:
        x, y = ([load(*windows[pair, lent, k], bins) for k in range(seg)] for lent in (False, pair > 0))
        tiles = [[powers[p, lent, k] for k in range(seg)] for p, lent in ((0, False), (pair, pair > 0))]
        loads.append([x, y] + [[load(array, array.shape[0] - 1, 1) for array in part] for part in tiles])
    rows, kept = arrays[0].shape[1], windows[0, False, 0][0]
    anywhere, in_hbm = pl.BlockSpec(memory_space=pl.ANY), pl.BlockSpec(memory_space=pltpu.HBM)
    operands = [sched, *arrays]
    aliases = {}
    if out is not None:
        aliases = {len(operands): 0}
        operands.append(out)
    kernel = functools.partial(cross_kernel, pairs, loads, samples, scale)
    if out is not None:
        kernel = functools.partial(drop_ref, len(operands) - 1, kernel)
    return pl.pallas_call(
        kernel,
        in_specs=[in_hbm if a is sched or a is kept else anywhere for a in operands],
        out_specs=anywhere,
        scratch_shapes=[
            pltpu.SMEM(sched.shape, jnp.int32),
            pltpu.VMEM((len(slots), bins, rows, width), jnp.bfloat16),
            pltpu.VMEM((len(pairs), 3, 2, chunk, width, width), jnp.bfloat16),
            pltpu.VMEM((width, width), jnp.float32),
            pltpu.SemaphoreType.DMA,
            pltpu.SemaphoreType.DMA((len(slots),)),
            pltpu.SemaphoreType.DMA((len(pairs), bins // chunk)),
        ],
        out_shape=jax.ShapeDtypeStruct(shape, jnp.bfloat16),
        input_output_aliases=aliases,
        compiler_params=pltpu.CompilerParams(vmem_limit_bytes=CROSS_VMEM),
        cost_estimate=pl.CostEstimate(
            flops=4 * len(pairs) * bins * seg * rows * width * width,
            bytes_accessed=4 * len(pairs) * bins * width * width,
            transcendentals=0,
        ),
    )(*operands)


def drop_ref(k, kernel, *refs):
    return kernel(*refs[:k], *refs[k + 1 :])


def body(signal, band, sched):
    seg_dev, length, width = signal.shape
    seg, chan = lax.axis_size("seg"), lax.axis_size("chan")
    segs = seg_dev * seg
    bins = BW // seg
    first, plan = message_plan(seg)
    table = dft_table(NB, length)
    cuts = early_spectra(first, seg, band.T, jnp.asarray(row_table(table)), signal)
    cuts += make_spectra(plan, seg, band.T, jnp.asarray(table), signal, cuts[0])

    def delivered(message, cut):
        pairs, lent, shift, _ = message
        away = pairs[0] if lent else 0
        if not away and not shift:
            return cut
        route = [(c * seg + s, (c - away) % chan * seg + (s + shift) % seg) for c in range(chan) for s in range(seg)]
        return lax.ppermute(cut, ("chan", "seg"), route)

    windows, powers = {}, {}
    scale = 1.0 / (segs * 0.375 * length) / LIFT**2
    shape = (1, PAIRS, 2, bins, width, width)
    out = None

    def deliver(message, cut, out=None):
        if out is not None:
            cut, out = lax.optimization_barrier((cut, out))
        pairs, lent, shift, powered = message
        array = delivered(message, cut)
        for i, pair in enumerate(pairs):
            windows[pair, lent, shift] = array, i * bins
            if powered:
                powers[pair, lent, shift] = array
        return out

    cuts = dict(zip(first + plan, cuts))
    for message, cut in cuts.items():
        if comes_after(message) is None:
            deliver(message, cut)
    for pairs in GROUPS:
        out = cross(pairs, seg, segs * length, scale, sched, windows, powers, shape, out)
        for message, cut in cuts.items():
            if comes_after(message) == pairs[-1]:
                out = deliver(message, cut, out)
    return out


def solution(mesh):
    in_specs = (P("seg", None, "chan"), P(), P("chan", None))
    out_specs = P("chan", None, None, "seg", None, None)
    return jax.shard_map(body, mesh=mesh, in_specs=in_specs, out_specs=out_specs, check_vma=False)
```

time: 62.6 us -> 58.2 us (0.930)
  the two profiles are of different devices: /device:TPU:0 before, /device:TPU:1 now
where the time goes in v3:
time: 58.2 us; the launch traced here: 57.1 us
  Pallas kernels  29.9 us (51%)
  starting transfers between devices  16.7 us (29%)
  waiting for transfers between devices  8.36 us (14%)
  local copies, waits for them, and re-layouts  1.89 us (3%)
    ppermute x8, starting transfers between devices, delivered(): return lax.ppermute(cut, ('chan', 'seg'), route)  16.7 us
    pallas_call x3, Pallas kernels, cross(): pl.pallas_call(kernel, in_specs=[in_hbm if a is sched or a is kept else a...  15.8 us
    pallas_call x1, Pallas kernels, make_spectra(): pl.pallas_call(functools.partial(spectra_kernel, plan, seg), in_specs=[pl...  8.41 us
    ppermute x8, waiting for transfers between devices, delivered(): return lax.ppermute(cut, ('chan', 'seg'), route)  8.36 us
    pallas_call x1, Pallas kernels, early_spectra(): pl.pallas_call(functools.partial(early_kernel, plan, seg), in_specs=[pl.B...  5.66 us
    unnamed x8, local copies, waits for them, and re-layouts  1.89 us
  transfers between devices with their start and end apart: 8, of which 2 were waited for; matrix products, arithmetic and copies ran while one was open for 0% of the time, Pallas kernels for 31%

profile of v3, /device:TPU:1, one launch (start us, length us, event | category | flops | bytes accessed | tf_op | source)
XLA Modules:
  0.0 57.1 jit_solution(3147577456345292598)
XLA Ops:
  0.0 5.7 %shard_map.55 = (bf16[65,16,256]{2,1,0:T(8,128)(2,1)}, bf16[33,16,256]{2,1,0:T(8,128)(2,1)}) custom-call(s32[4,16]{1,0:T(4,128)} %bitcast.1, f32[2,8,264,128]{3,2,1,0:T(8,128)} %constant.4.clone.rows_hbm, bf16[8,1024,256]{2,1,0:T(8,128)(2,1)} %signal_hbm.3), custom_call_target="tpu_custom_call" | custom-call | tf_op jit(solution)/shard_map/pallas_call | solution.py:129
  5.7 2.1 %collective-permute-start.2 = (bf16[65,16,256]{2,1,0:T(8,128)(2,1)}, bf16[65,16,256]{2,1,0:T(8,128)(2,1)S(1)}, u32[]{:S(2)}, u32[]{:S(2)}) collective-permute-start(bf16[65,16,256]{2,1,0:T(8,128)(2,1)} %get-tuple-element.18.early_hbm), channel_id=1, source_target_pairs={{0,1},{1,0},{2,3},{3,2},{4,5},{5,4},{6,7},{7,6},{8,9},{9,8},{10,11... | collective-permute-start | bytes 1597448 | tf_op jit(solution)/shard_map/ppermute | solution.py:357
  7.8 0.6 %collective-permute-start.7 = (bf16[33,16,256]{2,1,0:T(8,128)(2,1)}, bf16[33,16,256]{2,1,0:T(8,128)(2,1)S(1)}, u32[]{:S(2)}, u32[]{:S(2)}) collective-permute-start(bf16[33,16,256]{2,1,0:T(8,128)(2,1)} %get-tuple-element.29), channel_id=1, source_target_pairs={{0,31},{1,30},{2,1},{3,0},{4,3},{5,2},{6,5},{7,4},{8,7},{9,6},{10,... | collective-permute-start | bytes 811016 | tf_op jit(solution)/shard_map/ppermute | solution.py:357
  8.4 8.4 %shard_map.56 = (bf16[33,16,256]{2,1,0:T(8,128)(2,1)}, bf16[33,16,256]{2,1,0:T(8,128)(2,1)}, bf16[33,16,256]{2,1,0:T(8,128)(2,1)}, bf16[64,16,256]{2,1,0:T(8,128...) custom-call(s32[4,16]{1,0:T(4,128)} %bitcast.2, ...), custom_call_target="tpu_custom_call" | custom-call | flops 2147483648 | bytes 33554432 | tf_op jit(solution)/shard_map/pallas_call | solution.py:190
  16.8 4.1 %collective-permute-start.6 = (bf16[33,16,256]{2,1,0:T(8,128)(2,1)}, bf16[33,16,256]{2,1,0:T(8,128)(2,1)S(1)}, u32[]{:S(2)}, u32[]{:S(2)}) collective-permute-start(bf16[33,16,256]{2,1,0:T(8,128)(2,1)} %get-tuple-element.28), channel_id=1, source_target_pairs={{0,30},{1,31},{2,0},{3,1},{4,2},{5,3},{6,4},{7,5},{8,6},{9,7},{10,... | collective-permute-start | bytes 811016 | tf_op jit(solution)/shard_map/ppermute | solution.py:357
  20.9 1.2 %collective-permute-start = (bf16[64,16,256]{2,1,0:T(8,128)(2,1)}, bf16[64,16,256]{2,1,0:T(8,128)(2,1)S(1)}, u32[]{:S(2)}, u32[]{:S(2)}) collective-permute-start(bf16[64,16,256]{2,1,0:T(8,128)(2,1)} %get-tuple-element.20), channel_id=1, source_target_pairs={{0,1},{1,0},{2,3},{3,2},{4,5},{5,4},{6,7},{7,6},{8,9},{9,8},{10,11... | collective-permute-start | bytes 1572872 | tf_op jit(solution)/shard_map/ppermute | solution.py:357
  22.1 0.8 %collective-permute-start.1 = (bf16[33,16,256]{2,1,0:T(8,128)(2,1)}, bf16[33,16,256]{2,1,0:T(8,128)(2,1)S(1)}, u32[]{:S(2)}, u32[]{:S(2)}) collective-permute-start(bf16[33,16,256]{2,1,0:T(8,128)(2,1)} %get-tuple-element.21), channel_id=1, source_target_pairs={{0,28},{1,29},{2,30},{3,31},{4,0},{5,1},{6,2},{7,3},{8,4},{9,5},{1... | collective-permute-start | bytes 811016 | tf_op jit(solution)/shard_map/ppermute | solution.py:357
  22.9 0.0 collective-permute-done.2.refs_1_.refs_2_.refs_5_
  22.9 3.7 %collective-permute-start.4 = (bf16[33,16,256]{2,1,0:T(8,128)(2,1)}, bf16[33,16,256]{2,1,0:T(8,128)(2,1)S(1)}, u32[]{:S(2)}, u32[]{:S(2)}) collective-permute-start(bf16[33,16,256]{2,1,0:T(8,128)(2,1)} %get-tuple-element.24), channel_id=1, source_target_pairs={{0,26},{1,27},{2,28},{3,29},{4,30},{5,31},{6,0},{7,1},{8,2},{9,3},... | collective-permute-start | bytes 811016 | tf_op jit(solution)/shard_map/ppermute | solution.py:357
  26.6 0.0 copy-start
  26.6 1.2 %copy-done = bf16[129,16,256]{2,1,0:T(8,128)(2,1)S(1)} copy-done((bf16[129,16,256]{2,1,0:T(8,128)(2,1)S(1)}, bf16[129,16,256]{2,1,0:T(8,128)(2,1)}, u32[]{:S(2)}) %copy-start) | copy-done | bytes 1056792
  27.8 0.0 copy-start.1
  27.8 0.7 %copy-done.1 = s32[1,4]{1,0:T(1,128)S(1)} copy-done((s32[1,4]{1,0:T(1,128)S(1)}, s32[1,4]{1,0:T(1,128)}, u32[]{:S(2)}) %copy-start.1) | copy-done | bytes 40
  28.5 0.0 copy-start.3
  28.5 0.0 copy-start.2
  28.5 5.0 %shard_map.57.refs_5_ = bf16[1,4,2,32,256,256]{5,4,3,2,1,0:T(8,128)(2,1)} custom-call(s32[1,4]{1,0:T(1,128)S(1)} %copy-done.1, bf16[129,16,256]{2,1,0:T(8,128)(2,1)S(1)} %copy-done, bf16[65,16,256]{2,1,0:T(8,128)(2,1)S(1)} %collective-permute-done.2.refs_1_.refs_2_.refs_5_), custom_call_target="tpu_custom_call" | custom-call | flops 268435456 | bytes 8388608 | tf_op jit(solution)/shard_map/pallas_call | solution.py:313
  33.4 0.0 collective-permute-done.7.refs_4_
  33.5 0.0 copy-done.3
  33.5 1.0 %collective-permute-start.5 = (bf16[33,16,256]{2,1,0:T(8,128)(2,1)S(1)}, bf16[33,16,256]{2,1,0:T(8,128)(2,1)S(1)}, u32[]{:S(2)}, u32[]{:S(2)}) collective-permute-start(bf16[33,16,256]{2,1,0:T(8,128)(2,1)S(1)} %copy-done.3), channel_id=1, source_target_pairs={{0,27},{1,26},{2,29},{3,28},{4,31},{5,30},{6,1},{7,0},{8,3},{9,2},... | collective-permute-start | bytes 811016 | tf_op jit(solution)/shard_map/ppermute | solution.py:357
  34.4 0.0 collective-permute-done.6.refs_3_
  34.4 0.0 copy-done.2
  34.5 3.2 %collective-permute-start.3 = (bf16[33,16,256]{2,1,0:T(8,128)(2,1)S(1)}, bf16[33,16,256]{2,1,0:T(8,128)(2,1)S(1)}, u32[]{:S(2)}, u32[]{:S(2)}) collective-permute-start(bf16[33,16,256]{2,1,0:T(8,128)(2,1)S(1)} %copy-done.2), channel_id=1, source_target_pairs={{0,29},{1,28},{2,31},{3,30},{4,1},{5,0},{6,3},{7,2},{8,5},{9,4},{1... | collective-permute-start | bytes 811016 | tf_op jit(solution)/shard_map/ppermute | solution.py:357
  37.7 4.1 %shard_map.58.refs_8_ = bf16[1,4,2,32,256,256]{5,4,3,2,1,0:T(8,128)(2,1)} custom-call(s32[1,4]{1,0:T(1,128)S(1)} %copy-done.1, bf16[129,16,256]{2,1,0:T(8,128)(2,1)S(1)} %copy-done, bf16[65,16,256]{2,1,0:T(8,128)(2,1)S(1)} %collective-permute-done.2.refs_1_.refs_2_.refs_5_, ...), custom_call_target="tpu_custom_call", output_to_operand_aliasing={{}: (5, {})} | custom-call | flops 268435456 | bytes 8388608 | tf_op jit(solution)/shard_map/pallas_call | solution.py:313
  41.8 0.0 collective-permute-done.1.refs_3_
  41.8 0.0 collective-permute-done.4.refs_6_
  41.8 7.1 %collective-permute-done.refs_2_ = bf16[64,16,256]{2,1,0:T(8,128)(2,1)S(1)} collective-permute-done((bf16[64,16,256]{2,1,0:T(8,128)(2,1)}, bf16[64,16,256]{2,1,0:T(8,128)(2,1)S(1)}, u32[]{:S(2)}, u32[]{:S(2)}) %collective-permute-start) | collective-permute-done | bytes 524320 | tf_op jit(solution)/shard_map/ppermute | solution.py:357
  49.0 0.0 collective-permute-done.5.refs_7_
  49.0 1.2 %collective-permute-done.3.refs_4_ = bf16[33,16,256]{2,1,0:T(8,128)(2,1)S(1)} collective-permute-done((bf16[33,16,256]{2,1,0:T(8,128)(2,1)S(1)}, bf16[33,16,256]{2,1,0:T(8,128)(2,1)S(1)}, u32[]{:S(2)}, u32[]{:S(2)}) %collective-permute-start.3) | collective-permute-done | bytes 270368 | tf_op jit(solution)/shard_map/ppermute | solution.py:357
  50.2 6.7 %shard_map.59 = bf16[1,4,2,32,256,256]{5,4,3,2,1,0:T(8,128)(2,1)} custom-call(s32[1,4]{1,0:T(1,128)S(1)} %copy-done.1, bf16[129,16,256]{2,1,0:T(8,128)(2,1)S(1)} %copy-done, bf16[64,16,256]{2,1,0:T(8,128)(2,1)S(1)} %collective-permute-done.refs_2_, bf16[33,16,256]{2,1,0:T(8,128)(2,1)S(1)} %collective-permute-done.1.refs_3_, ...), custom_call_target="tpu_custom_call", output_to_operand_aliasing={{}: (8, {})} | custom-call | flops 536870912 | bytes 16777216 | tf_op jit(solution)/shard_map/pallas_call | solution.py:313
Async XLA Ops:
  5.7 17.2 %collective-permute-start.2 = (bf16[65,16,256]{2,1,0:T(8,128)(2,1)}, bf16[65,16,256]{2,1,0:T(8,128)(2,1)S(1)}, u32[]{:S(2)}, u32[]{:S(2)}) collective-permute-start(bf16[65,16,256]{2,1,0:T(8,128)(2,1)} %get-tuple-element.18.early_hbm), channel_id=1, source_target_pairs={{0,1},{1,0},{2,3},{3,2},{4,5},{5,4},{6,7},{7,6},{8,9},{9,8},{10,11... | collective-permute-start | bytes 1597448 | tf_op jit(solution)/shard_map/ppermute | solution.py:357
  7.8 25.7 %collective-permute-start.7 = (bf16[33,16,256]{2,1,0:T(8,128)(2,1)}, bf16[33,16,256]{2,1,0:T(8,128)(2,1)S(1)}, u32[]{:S(2)}, u32[]{:S(2)}) collective-permute-start(bf16[33,16,256]{2,1,0:T(8,128)(2,1)} %get-tuple-element.29), channel_id=1, source_target_pairs={{0,31},{1,30},{2,1},{3,0},{4,3},{5,2},{6,5},{7,4},{8,7},{9,6},{10,... | collective-permute-start | bytes 811016 | tf_op jit(solution)/shard_map/ppermute | solution.py:357
  16.8 17.6 %collective-permute-start.6 = (bf16[33,16,256]{2,1,0:T(8,128)(2,1)}, bf16[33,16,256]{2,1,0:T(8,128)(2,1)S(1)}, u32[]{:S(2)}, u32[]{:S(2)}) collective-permute-start(bf16[33,16,256]{2,1,0:T(8,128)(2,1)} %get-tuple-element.28), channel_id=1, source_target_pairs={{0,30},{1,31},{2,0},{3,1},{4,2},{5,3},{6,4},{7,5},{8,6},{9,7},{10,... | collective-permute-start | bytes 811016 | tf_op jit(solution)/shard_map/ppermute | solution.py:357
  20.9 28.1 %collective-permute-start = (bf16[64,16,256]{2,1,0:T(8,128)(2,1)}, bf16[64,16,256]{2,1,0:T(8,128)(2,1)S(1)}, u32[]{:S(2)}, u32[]{:S(2)}) collective-permute-start(bf16[64,16,256]{2,1,0:T(8,128)(2,1)} %get-tuple-element.20), channel_id=1, source_target_pairs={{0,1},{1,0},{2,3},{3,2},{4,5},{5,4},{6,7},{7,6},{8,9},{9,8},{10,11... | collective-permute-start | bytes 1572872 | tf_op jit(solution)/shard_map/ppermute | solution.py:357
  22.1 19.7 %collective-permute-start.1 = (bf16[33,16,256]{2,1,0:T(8,128)(2,1)}, bf16[33,16,256]{2,1,0:T(8,128)(2,1)S(1)}, u32[]{:S(2)}, u32[]{:S(2)}) collective-permute-start(bf16[33,16,256]{2,1,0:T(8,128)(2,1)} %get-tuple-element.21), channel_id=1, source_target_pairs={{0,28},{1,29},{2,30},{3,31},{4,0},{5,1},{6,2},{7,3},{8,4},{9,5},{1... | collective-permute-start | bytes 811016 | tf_op jit(solution)/shard_map/ppermute | solution.py:357
  22.9 18.9 %collective-permute-start.4 = (bf16[33,16,256]{2,1,0:T(8,128)(2,1)}, bf16[33,16,256]{2,1,0:T(8,128)(2,1)S(1)}, u32[]{:S(2)}, u32[]{:S(2)}) collective-permute-start(bf16[33,16,256]{2,1,0:T(8,128)(2,1)} %get-tuple-element.24), channel_id=1, source_target_pairs={{0,26},{1,27},{2,28},{3,29},{4,30},{5,31},{6,0},{7,1},{8,2},{9,3},... | collective-permute-start | bytes 811016 | tf_op jit(solution)/shard_map/ppermute | solution.py:357
  26.6 1.2 %copy-start = (bf16[129,16,256]{2,1,0:T(8,128)(2,1)S(1)}, bf16[129,16,256]{2,1,0:T(8,128)(2,1)}, u32[]{:S(2)}) copy-start(bf16[129,16,256]{2,1,0:T(8,128)(2,1)} %get-tuple-element.19.refs_0_.refs_1_) | copy-start | bytes 3170308
  27.8 0.7 %copy-start.1 = (s32[1,4]{1,0:T(1,128)S(1)}, s32[1,4]{1,0:T(1,128)}, u32[]{:S(2)}) copy-start(s32[1,4]{1,0:T(1,128)} %refs_0_.3) | copy-start | bytes 52
  28.5 5.0 %copy-start.3 = (bf16[33,16,256]{2,1,0:T(8,128)(2,1)S(1)}, bf16[33,16,256]{2,1,0:T(8,128)(2,1)}, u32[]{:S(2)}) copy-start(bf16[33,16,256]{2,1,0:T(8,128)(2,1)} %get-tuple-element.27) | copy-start | bytes 811012
  28.5 6.0 %copy-start.2 = (bf16[33,16,256]{2,1,0:T(8,128)(2,1)S(1)}, bf16[33,16,256]{2,1,0:T(8,128)(2,1)}, u32[]{:S(2)}) copy-start(bf16[33,16,256]{2,1,0:T(8,128)(2,1)} %get-tuple-element.23) | copy-start | bytes 811012
  33.5 15.5 %collective-permute-start.5 = (bf16[33,16,256]{2,1,0:T(8,128)(2,1)S(1)}, bf16[33,16,256]{2,1,0:T(8,128)(2,1)S(1)}, u32[]{:S(2)}, u32[]{:S(2)}) collective-permute-start(bf16[33,16,256]{2,1,0:T(8,128)(2,1)S(1)} %copy-done.3), channel_id=1, source_target_pairs={{0,27},{1,26},{2,29},{3,28},{4,31},{5,30},{6,1},{7,0},{8,3},{9,2},... | collective-permute-start | bytes 811016 | tf_op jit(solution)/shard_map/ppermute | solution.py:357
  34.5 15.7 %collective-permute-start.3 = (bf16[33,16,256]{2,1,0:T(8,128)(2,1)S(1)}, bf16[33,16,256]{2,1,0:T(8,128)(2,1)S(1)}, u32[]{:S(2)}, u32[]{:S(2)}) collective-permute-start(bf16[33,16,256]{2,1,0:T(8,128)(2,1)S(1)} %copy-done.2), channel_id=1, source_target_pairs={{0,29},{1,28},{2,31},{3,30},{4,1},{5,0},{6,3},{7,2},{8,5},{9,4},{1... | collective-permute-start | bytes 811016 | tf_op jit(solution)/shard_map/ppermute | solution.py:357

commit v4 on v3

--- a/solution.py
+++ b/solution.py
@@ -16,6 +16,7 @@
 LIFT = 1024.0
 CROSS_VMEM = 24 << 20
 GROUPS = ((0,), (1,), (2, 3))
+CHUNK = 8
 
 
 def dft_table(nbins, length):
@@ -82,10 +83,11 @@
     for w, start in enumerate(windows):
         aligned = pl.multiple_of(start // 8 * 8, 8)
         row_copies.append(pltpu.make_async_copy(rows_hbm.at[:, :, pl.ds(aligned, bins + 8), :], rows_held.at[w], row_sem.at[w]))
-    signal_copy = pltpu.make_async_copy(signal_hbm, signal, signal_sem)
+    signal_copies = [pltpu.make_async_copy(signal_hbm.at[s], signal.at[s], signal_sem.at[s]) for s in range(segs)]
     for copy in row_copies:
         copy.start()
-    signal_copy.start()
+    for copy in signal_copies:
+        copy.start()
     for copy in row_copies:
         copy.wait()
     pieces = []
@@ -94,7 +96,8 @@
             chunks = [rows_held[w, r, k, pl.ds(lax.rem(start, 8), bins), :] for k in range(rows_held.shape[2])]
             pieces.append(jnp.concatenate(chunks, axis=1))
     table = jnp.concatenate(pieces, axis=0).astype(jnp.bfloat16)
-    signal_copy.wait()
+    for copy in signal_copies:
+        copy.wait()
     power = jnp.zeros((8, width), jnp.float32)
     for s in range(segs):
         spectrum = jnp.dot(table, signal[s], preferred_element_type=jnp.float32)
@@ -108,7 +111,7 @@
     total = len(windows) * bins
     cut[total] = power_tile(power, rows)
     for h in range(width // LANES):
-        cut[:total, :, h * LANES : (h + 1) * LANES] = raw[h].reshape(total, rows, LANES).astype(jnp.bfloat16)
+        cut[:total, :, h * LANES : (h + 1) * LANES] = raw[h, : total * rows].reshape(total, rows, LANES).astype(jnp.bfloat16)
     copies, at = [], 0
     for (pairs, _, _, _), out in zip(plan, outs):
         size = len(pairs) * bins
@@ -134,10 +137,10 @@
         scratch_shapes=[
             pltpu.VMEM((n, 2, length // LANES, bins + 8, LANES), jnp.float32),
             pltpu.VMEM(signal.shape, jnp.bfloat16),
-            pltpu.VMEM((width // LANES, n * bins * rows, LANES), jnp.float32),
+            pltpu.VMEM((width // LANES, (n * bins + 1) * rows, LANES), jnp.float32),
             pltpu.VMEM((n * bins + 1, rows, width), jnp.bfloat16),
             pltpu.SemaphoreType.DMA((n,)),
-            pltpu.SemaphoreType.DMA,
+            pltpu.SemaphoreType.DMA((segs,)),
             pltpu.SemaphoreType.DMA((2 * len(plan),)),
         ],
         compiler_params=pltpu.CompilerParams(vmem_limit_bytes=56 << 20),
@@ -152,21 +155,23 @@
     rows = 2 * segs
     bins = BW // seg
     table_copy = pltpu.make_async_copy(table_hbm, table, table_sem)
-    signal_copy = pltpu.make_async_copy(signal_hbm, signal, signal_sem)
+    signal_copies = [pltpu.make_async_copy(signal_hbm.at[s], signal.at[s], signal_sem.at[s]) for s in range(segs)]
     power_copy = pltpu.make_async_copy(early_hbm.at[pl.ds(early_hbm.shape[0] - 1, 1)], spectra.at[pl.ds(nbins, 1)], power_sem)
     table_copy.start()
     power_copy.start()
-    signal_copy.start()
+    for copy in signal_copies:
+        copy.start()
     table_copy.wait()
     power_copy.wait()
-    signal_copy.wait()
+    for copy in signal_copies:
+        copy.wait()
     for s in range(segs):
         spectrum = jnp.dot(table[...], signal[s], preferred_element_type=jnp.float32)
         for r in range(2):
             for h in range(width // LANES):
                 raw[h, pl.ds(r * segs + s, nbins, stride=rows), :] = spectrum[r * nbins : (r + 1) * nbins, h * LANES : (h + 1) * LANES]
     for h in range(width // LANES):
-        spectra[:nbins, :, h * LANES : (h + 1) * LANES] = raw[h].reshape(nbins, rows, LANES).astype(jnp.bfloat16)
+        spectra[:nbins, :, h * LANES : (h + 1) * LANES] = raw[h, : nbins * rows].reshape(nbins, rows, LANES).astype(jnp.bfloat16)
     copies = []
     for (pairs, lent, shift, powered), out in zip(plan, outs):
         pieces = [(first_bin(band_ref, pair, lent, shift, seg), bins) for pair in pairs] + [(nbins, 1)] * powered
@@ -195,10 +200,10 @@
         scratch_shapes=[
             pltpu.VMEM(table.shape, jnp.bfloat16),
             pltpu.VMEM(signal.shape, jnp.bfloat16),
-            pltpu.VMEM((width // LANES, nbins * rows, LANES), jnp.float32),
+            pltpu.VMEM((width // LANES, (nbins + 1) * rows, LANES), jnp.float32),
             pltpu.VMEM((nbins + 1, rows, width), jnp.bfloat16),
             pltpu.SemaphoreType.DMA,
-            pltpu.SemaphoreType.DMA,
+            pltpu.SemaphoreType.DMA((segs,)),
             pltpu.SemaphoreType.DMA,
             pltpu.SemaphoreType.DMA((sum(len(m[0]) + m[3] for m in plan),)),
         ],
@@ -220,37 +225,51 @@
     return lax.rsqrt(power / samples + 1e-06)
 
 
+def chunks_of(bins, lead, trail):
+    sizes = [min(CHUNK, bins - f) for f in range(0, bins, CHUNK)]
+    if lead and sizes[0] > 2:
+        sizes[:1] = [2, sizes[0] - 2]
+    if trail and sizes[-1] > 2:
+        sizes[-1:] = [sizes[-1] - sizes[-1] // 2, sizes[-1] // 2]
+    return [(sum(sizes[:c]), size) for c, size in enumerate(sizes)]
+
+
 def cross_kernel(pairs, loads, samples, scale, sched_hbm, *refs):
     *arrays, out, sched_ref, held, ring, weight, sched_sem, in_sem, out_sem = refs
     sched_copy = pltpu.make_async_copy(sched_hbm, sched_ref, sched_sem)
     sched_copy.start()
     width = held.shape[-1]
-    _, depth, _, chunk = ring.shape[:4]
-    bins = out.shape[3]
-    steps = bins // chunk
+    depth = ring.shape[1]
+    chunks = [chunks_of(out.shape[3], i == 0, i == len(pairs) - 1) for i in range(len(pairs))]
     in_copies, out_copies, zero_copies = {}, [], []
     for load in loads:
         for array, first, size, slot in sum(load, []):
             if slot not in in_copies:
                 in_copies[slot] = pltpu.make_async_copy(arrays[array].at[pl.ds(first, size)], held.at[slot, pl.ds(0, size)], in_sem.at[slot])
     for i, pair in enumerate(pairs):
-        for source, copies in ((lambda c: c % depth, out_copies), (lambda c: 0, zero_copies)):
+        for slots, copies in ((depth, out_copies), (1, zero_copies)):
             copies.append(
                 [
-                    pltpu.make_async_copy(ring.at[i, source(c)], out.at[0, pair, :, pl.ds(c * chunk, chunk)], out_sem.at[i, c])
-                    for c in range(steps)
+                    pltpu.make_async_copy(
+                        ring.at[i, c % slots, :, pl.ds(0, size)], out.at[0, pair, :, pl.ds(first, size)], out_sem.at[i, c]
+                    )
+                    for c, (first, size) in enumerate(chunks[i])
                 ]
             )
-    for copy in in_copies.values():
-        copy.start()
+    fresh, known = [], set()
+    for load in loads:
+        fresh.append([slot for *_, slot in sum(load, []) if slot not in known])
+        fresh[-1] = list(dict.fromkeys(fresh[-1]))
+        known.update(fresh[-1])
+    for slot in fresh[0]:
+        in_copies[slot].start()
     sched_copy.wait()
-    waited = set()
     for i, pair in enumerate(pairs):
         x_loads, y_loads, x_power, y_power = ([slot for _, _, _, slot in part] for part in loads[i])
-        for slot in x_loads + y_loads + x_power + y_power:
-            if slot not in waited:
-                in_copies[slot].wait()
-                waited.add(slot)
+        for slot in fresh[i]:
+            in_copies[slot].wait()
+        for slot in fresh[i + 1] if i + 1 < len(pairs) else []:
+            in_copies[slot].start()
         live = sched_ref[0, pair]
 
         @pl.when(live == 0)
@@ -258,17 +277,17 @@
             ring[i, 0] = jnp.zeros(ring.shape[2:], ring.dtype)
             for c, copy in enumerate(zero_copies[i]):
                 copy.start()
-            for copy in zero_copies[i][: max(steps - depth, 0)]:
+            for copy in zero_copies[i][:-depth]:
                 copy.wait()
 
         @pl.when(live != 0)
         def _(i=i, x_loads=x_loads, y_loads=y_loads, x_power=x_power, y_power=y_power):
             by_row = jnp.broadcast_to(inv_rms_of([held[k, 0] for k in x_power], samples) * scale, (width, width)).T
             weight[...] = by_row * inv_rms_of([held[k, 0] for k in y_power], samples)
-            for c in range(steps):
+            for c, (first, size) in enumerate(chunks[i]):
                 if c >= depth:
                     out_copies[i][c - depth].wait()
-                for f in range(c * chunk, (c + 1) * chunk):
+                for f in range(first, first + size):
                     x = jnp.concatenate([held[k, f] for k in x_loads], axis=0)
                     y = jnp.concatenate([held[k, f] for k in y_loads], axis=0)
                     y_turned = jnp.concatenate([turned(held[k, f]) for k in y_loads], axis=0)
@@ -276,17 +295,16 @@
                     product = lax.dot_general(x, partner, (((0,), (0,)), ((), ())), preferred_element_type=jnp.float32)
                     for r in range(2):
                         part = product[:, r * width : (r + 1) * width] * weight[...]
-                        ring[i, c % depth, r, f - c * chunk] = part.astype(ring.dtype)
+                        ring[i, c % depth, r, f - first] = part.astype(ring.dtype)
                 out_copies[i][c].start()
 
     for copies in out_copies:
-        for copy in copies[max(steps - depth, 0) :]:
+        for copy in copies[-depth:]:
             copy.wait()
 
 
 def cross(pairs, seg, samples, scale, sched, windows, powers, shape, out):
     bins, width = shape[3], shape[4]
-    chunk = min(8, bins)
     arrays, slots, loads = [], {}, []
 
     def load(array, first, size):
@@ -317,11 +335,11 @@
         scratch_shapes=[
             pltpu.SMEM(sched.shape, jnp.int32),
             pltpu.VMEM((len(slots), bins, rows, width), jnp.bfloat16),
-            pltpu.VMEM((len(pairs), 3, 2, chunk, width, width), jnp.bfloat16),
+            pltpu.VMEM((len(pairs), 3, 2, min(CHUNK, bins), width, width), jnp.bfloat16),
             pltpu.VMEM((width, width), jnp.float32),
             pltpu.SemaphoreType.DMA,
             pltpu.SemaphoreType.DMA((len(slots),)),
-            pltpu.SemaphoreType.DMA((len(pairs), bins // chunk)),
+            pltpu.SemaphoreType.DMA((len(pairs), bins // min(CHUNK, bins) + 2)),
         ],
         out_shape=jax.ShapeDtypeStruct(shape, jnp.bfloat16),
         input_output_aliases=aliases,

time: 58.2 us -> 58 us (level)
  the two profiles are of different devices: /device:TPU:1 before, /device:TPU:0 now
where the time goes in v4:
time: 58 us; the launch traced here: 57.3 us
  Pallas kernels  30.9 us (53%)
  starting transfers between devices  17.4 us (30%)
  waiting for transfers between devices  6.98 us (12%)
  local copies, waits for them, and re-layouts  1.89 us (3%)
    ppermute x8, starting transfers between devices, delivered(): return lax.ppermute(cut, ('chan', 'seg'), route)  17.4 us
    pallas_call x3, Pallas kernels, cross(): pl.pallas_call(kernel, in_specs=[in_hbm if a is sched or a is kept else a...  16.7 us
    pallas_call x1, Pallas kernels, make_spectra(): pl.pallas_call(functools.partial(spectra_kernel, plan, seg), in_specs=[pl...  8.42 us
    ppermute x8, waiting for transfers between devices, delivered(): return lax.ppermute(cut, ('chan', 'seg'), route)  6.98 us
    pallas_call x1, Pallas kernels, early_spectra(): pl.pallas_call(functools.partial(early_kernel, plan, seg), in_specs=[pl.B...  5.72 us
    unnamed x8, local copies, waits for them, and re-layouts  1.89 us
  transfers between devices with their start and end apart: 8, of which 3 were waited for; matrix products, arithmetic and copies ran while one was open for 0% of the time, Pallas kernels for 30%

profile of v4, /device:TPU:0, one launch (start us, length us, event | category | flops | bytes accessed | tf_op | source)
XLA Modules:
  0.0 57.3 jit_solution(1958520055978569813)
XLA Ops:
  0.0 5.7 %shard_map.55 = (bf16[65,16,256]{2,1,0:T(8,128)(2,1)}, bf16[33,16,256]{2,1,0:T(8,128)(2,1)}) custom-call(s32[4,16]{1,0:T(4,128)} %bitcast.1, f32[2,8,264,128]{3,2,1,0:T(8,128)} %constant.4.clone.rows_hbm, bf16[8,1024,256]{2,1,0:T(8,128)(2,1)} %signal_hbm.3), custom_call_target="tpu_custom_call" | custom-call | tf_op jit(solution)/shard_map/pallas_call | solution.py:132
  5.7 3.0 %collective-permute-start.2 = (bf16[65,16,256]{2,1,0:T(8,128)(2,1)}, bf16[65,16,256]{2,1,0:T(8,128)(2,1)S(1)}, u32[]{:S(2)}, u32[]{:S(2)}) collective-permute-start(bf16[65,16,256]{2,1,0:T(8,128)(2,1)} %get-tuple-element.18.early_hbm), channel_id=1, source_target_pairs={{0,1},{1,0},{2,3},{3,2},{4,5},{5,4},{6,7},{7,6},{8,9},{9,8},{10,11... | collective-permute-start | bytes 1597448 | tf_op jit(solution)/shard_map/ppermute | solution.py:375
  8.7 3.7 %collective-permute-start.7 = (bf16[33,16,256]{2,1,0:T(8,128)(2,1)}, bf16[33,16,256]{2,1,0:T(8,128)(2,1)S(1)}, u32[]{:S(2)}, u32[]{:S(2)}) collective-permute-start(bf16[33,16,256]{2,1,0:T(8,128)(2,1)} %get-tuple-element.29), channel_id=1, source_target_pairs={{0,31},{1,30},{2,1},{3,0},{4,3},{5,2},{6,5},{7,4},{8,7},{9,6},{10,... | collective-permute-start | bytes 811016 | tf_op jit(solution)/shard_map/ppermute | solution.py:375
  12.4 8.4 %shard_map.56 = (bf16[33,16,256]{2,1,0:T(8,128)(2,1)}, bf16[33,16,256]{2,1,0:T(8,128)(2,1)}, bf16[33,16,256]{2,1,0:T(8,128)(2,1)}, bf16[64,16,256]{2,1,0:T(8,128...) custom-call(s32[4,16]{1,0:T(4,128)} %bitcast.2, ...), custom_call_target="tpu_custom_call" | custom-call | flops 2147483648 | bytes 33554432 | tf_op jit(solution)/shard_map/pallas_call | solution.py:195
  20.8 1.2 %collective-permute-start.6 = (bf16[33,16,256]{2,1,0:T(8,128)(2,1)}, bf16[33,16,256]{2,1,0:T(8,128)(2,1)S(1)}, u32[]{:S(2)}, u32[]{:S(2)}) collective-permute-start(bf16[33,16,256]{2,1,0:T(8,128)(2,1)} %get-tuple-element.28), channel_id=1, source_target_pairs={{0,30},{1,31},{2,0},{3,1},{4,2},{5,3},{6,4},{7,5},{8,6},{9,7},{10,... | collective-permute-start | bytes 811016 | tf_op jit(solution)/shard_map/ppermute | solution.py:375
  22.0 1.5 %collective-permute-start = (bf16[64,16,256]{2,1,0:T(8,128)(2,1)}, bf16[64,16,256]{2,1,0:T(8,128)(2,1)S(1)}, u32[]{:S(2)}, u32[]{:S(2)}) collective-permute-start(bf16[64,16,256]{2,1,0:T(8,128)(2,1)} %get-tuple-element.20), channel_id=1, source_target_pairs={{0,1},{1,0},{2,3},{3,2},{4,5},{5,4},{6,7},{7,6},{8,9},{9,8},{10,11... | collective-permute-start | bytes 1572872 | tf_op jit(solution)/shard_map/ppermute | solution.py:375
  23.5 0.5 collective-permute-start.1
  24.0 0.7 %collective-permute-done.2.refs_1_.refs_2_.refs_5_ = bf16[65,16,256]{2,1,0:T(8,128)(2,1)S(1)} collective-permute-done((bf16[65,16,256]{2,1,0:T(8,128)(2,1)}, bf16[65,16,256]{2,1,0:T(8,128)(2,1)S(1)}, u32[]{:S(2)}, u32[]{:S(2)}) %collective-permute-start.2) | collective-permute-done | bytes 532512 | tf_op jit(solution)/shard_map/ppermute | solution.py:375
  24.8 1.6 %collective-permute-start.4 = (bf16[33,16,256]{2,1,0:T(8,128)(2,1)}, bf16[33,16,256]{2,1,0:T(8,128)(2,1)S(1)}, u32[]{:S(2)}, u32[]{:S(2)}) collective-permute-start(bf16[33,16,256]{2,1,0:T(8,128)(2,1)} %get-tuple-element.24), channel_id=1, source_target_pairs={{0,26},{1,27},{2,28},{3,29},{4,30},{5,31},{6,0},{7,1},{8,2},{9,3},... | collective-permute-start | bytes 811016 | tf_op jit(solution)/shard_map/ppermute | solution.py:375
  26.4 0.0 copy-start
  26.4 1.2 %copy-done = bf16[129,16,256]{2,1,0:T(8,128)(2,1)S(1)} copy-done((bf16[129,16,256]{2,1,0:T(8,128)(2,1)S(1)}, bf16[129,16,256]{2,1,0:T(8,128)(2,1)}, u32[]{:S(2)}) %copy-start) | copy-done | bytes 1056792
  27.6 0.0 copy-start.1
  27.6 0.7 %copy-done.1 = s32[1,4]{1,0:T(1,128)S(1)} copy-done((s32[1,4]{1,0:T(1,128)S(1)}, s32[1,4]{1,0:T(1,128)}, u32[]{:S(2)}) %copy-start.1) | copy-done | bytes 40
  28.2 0.0 copy-start.3
  28.2 0.0 copy-start.2
  28.2 4.1 %shard_map.57.refs_5_ = bf16[1,4,2,32,256,256]{5,4,3,2,1,0:T(8,128)(2,1)} custom-call(s32[1,4]{1,0:T(1,128)S(1)} %copy-done.1, bf16[129,16,256]{2,1,0:T(8,128)(2,1)S(1)} %copy-done, bf16[65,16,256]{2,1,0:T(8,128)(2,1)S(1)} %collective-permute-done.2.refs_1_.refs_2_.refs_5_), custom_call_target="tpu_custom_call" | custom-call | flops 268435456 | bytes 8388608 | tf_op jit(solution)/shard_map/pallas_call | solution.py:331
  32.3 0.0 collective-permute-done.7.refs_4_
  32.3 0.0 copy-done.3
  32.3 2.5 %collective-permute-start.5 = (bf16[33,16,256]{2,1,0:T(8,128)(2,1)S(1)}, bf16[33,16,256]{2,1,0:T(8,128)(2,1)S(1)}, u32[]{:S(2)}, u32[]{:S(2)}) collective-permute-start(bf16[33,16,256]{2,1,0:T(8,128)(2,1)S(1)} %copy-done.3), channel_id=1, source_target_pairs={{0,27},{1,26},{2,29},{3,28},{4,31},{5,30},{6,1},{7,0},{8,3},{9,2},... | collective-permute-start | bytes 811016 | tf_op jit(solution)/shard_map/ppermute | solution.py:375
  34.9 0.0 collective-permute-done.6.refs_3_
  34.9 0.0 copy-done.2
  34.9 3.4 %collective-permute-start.3 = (bf16[33,16,256]{2,1,0:T(8,128)(2,1)S(1)}, bf16[33,16,256]{2,1,0:T(8,128)(2,1)S(1)}, u32[]{:S(2)}, u32[]{:S(2)}) collective-permute-start(bf16[33,16,256]{2,1,0:T(8,128)(2,1)S(1)} %copy-done.2), channel_id=1, source_target_pairs={{0,29},{1,28},{2,31},{3,30},{4,1},{5,0},{6,3},{7,2},{8,5},{9,4},{1... | collective-permute-start | bytes 811016 | tf_op jit(solution)/shard_map/ppermute | solution.py:375
  38.3 4.9 %shard_map.58.refs_8_ = bf16[1,4,2,32,256,256]{5,4,3,2,1,0:T(8,128)(2,1)} custom-call(s32[1,4]{1,0:T(1,128)S(1)} %copy-done.1, bf16[129,16,256]{2,1,0:T(8,128)(2,1)S(1)} %copy-done, bf16[65,16,256]{2,1,0:T(8,128)(2,1)S(1)} %collective-permute-done.2.refs_1_.refs_2_.refs_5_, ...), custom_call_target="tpu_custom_call", output_to_operand_aliasing={{}: (5, {})} | custom-call | flops 268435456 | bytes 8388608 | tf_op jit(solution)/shard_map/pallas_call | solution.py:331
  43.1 0.0 collective-permute-done.1.refs_3_
  43.1 0.0 collective-permute-done.4.refs_6_
  43.1 0.0 collective-permute-done.refs_2_
  43.2 3.7 %collective-permute-done.5.refs_7_ = bf16[33,16,256]{2,1,0:T(8,128)(2,1)S(1)} collective-permute-done((bf16[33,16,256]{2,1,0:T(8,128)(2,1)S(1)}, bf16[33,16,256]{2,1,0:T(8,128)(2,1)S(1)}, u32[]{:S(2)}, u32[]{:S(2)}) %collective-permute-start.5) | collective-permute-done | bytes 270368 | tf_op jit(solution)/shard_map/ppermute | solution.py:375
  46.8 2.6 %collective-permute-done.3.refs_4_ = bf16[33,16,256]{2,1,0:T(8,128)(2,1)S(1)} collective-permute-done((bf16[33,16,256]{2,1,0:T(8,128)(2,1)S(1)}, bf16[33,16,256]{2,1,0:T(8,128)(2,1)S(1)}, u32[]{:S(2)}, u32[]{:S(2)}) %collective-permute-start.3) | collective-permute-done | bytes 270368 | tf_op jit(solution)/shard_map/ppermute | solution.py:375
  49.4 7.8 %shard_map.59 = bf16[1,4,2,32,256,256]{5,4,3,2,1,0:T(8,128)(2,1)} custom-call(s32[1,4]{1,0:T(1,128)S(1)} %copy-done.1, bf16[129,16,256]{2,1,0:T(8,128)(2,1)S(1)} %copy-done, bf16[64,16,256]{2,1,0:T(8,128)(2,1)S(1)} %collective-permute-done.refs_2_, bf16[33,16,256]{2,1,0:T(8,128)(2,1)S(1)} %collective-permute-done.1.refs_3_, ...), custom_call_target="tpu_custom_call", output_to_operand_aliasing={{}: (8, {})} | custom-call | flops 536870912 | bytes 16777216 | tf_op jit(solution)/shard_map/pallas_call | solution.py:331
Async XLA Ops:
  5.7 19.0 %collective-permute-start.2 = (bf16[65,16,256]{2,1,0:T(8,128)(2,1)}, bf16[65,16,256]{2,1,0:T(8,128)(2,1)S(1)}, u32[]{:S(2)}, u32[]{:S(2)}) collective-permute-start(bf16[65,16,256]{2,1,0:T(8,128)(2,1)} %get-tuple-element.18.early_hbm), channel_id=1, source_target_pairs={{0,1},{1,0},{2,3},{3,2},{4,5},{5,4},{6,7},{7,6},{8,9},{9,8},{10,11... | collective-permute-start | bytes 1597448 | tf_op jit(solution)/shard_map/ppermute | solution.py:375
  8.7 23.6 %collective-permute-start.7 = (bf16[33,16,256]{2,1,0:T(8,128)(2,1)}, bf16[33,16,256]{2,1,0:T(8,128)(2,1)S(1)}, u32[]{:S(2)}, u32[]{:S(2)}) collective-permute-start(bf16[33,16,256]{2,1,0:T(8,128)(2,1)} %get-tuple-element.29), channel_id=1, source_target_pairs={{0,31},{1,30},{2,1},{3,0},{4,3},{5,2},{6,5},{7,4},{8,7},{9,6},{10,... | collective-permute-start | bytes 811016 | tf_op jit(solution)/shard_map/ppermute | solution.py:375
  20.8 14.0 %collective-permute-start.6 = (bf16[33,16,256]{2,1,0:T(8,128)(2,1)}, bf16[33,16,256]{2,1,0:T(8,128)(2,1)S(1)}, u32[]{:S(2)}, u32[]{:S(2)}) collective-permute-start(bf16[33,16,256]{2,1,0:T(8,128)(2,1)} %get-tuple-element.28), channel_id=1, source_target_pairs={{0,30},{1,31},{2,0},{3,1},{4,2},{5,3},{6,4},{7,5},{8,6},{9,7},{10,... | collective-permute-start | bytes 811016 | tf_op jit(solution)/shard_map/ppermute | solution.py:375
  22.0 21.1 %collective-permute-start = (bf16[64,16,256]{2,1,0:T(8,128)(2,1)}, bf16[64,16,256]{2,1,0:T(8,128)(2,1)S(1)}, u32[]{:S(2)}, u32[]{:S(2)}) collective-permute-start(bf16[64,16,256]{2,1,0:T(8,128)(2,1)} %get-tuple-element.20), channel_id=1, source_target_pairs={{0,1},{1,0},{2,3},{3,2},{4,5},{5,4},{6,7},{7,6},{8,9},{9,8},{10,11... | collective-permute-start | bytes 1572872 | tf_op jit(solution)/shard_map/ppermute | solution.py:375
  23.5 19.6 %collective-permute-start.1 = (bf16[33,16,256]{2,1,0:T(8,128)(2,1)}, bf16[33,16,256]{2,1,0:T(8,128)(2,1)S(1)}, u32[]{:S(2)}, u32[]{:S(2)}) collective-permute-start(bf16[33,16,256]{2,1,0:T(8,128)(2,1)} %get-tuple-element.21), channel_id=1, source_target_pairs={{0,28},{1,29},{2,30},{3,31},{4,0},{5,1},{6,2},{7,3},{8,4},{9,5},{1... | collective-permute-start | bytes 811016 | tf_op jit(solution)/shard_map/ppermute | solution.py:375
  24.8 18.4 %collective-permute-start.4 = (bf16[33,16,256]{2,1,0:T(8,128)(2,1)}, bf16[33,16,256]{2,1,0:T(8,128)(2,1)S(1)}, u32[]{:S(2)}, u32[]{:S(2)}) collective-permute-start(bf16[33,16,256]{2,1,0:T(8,128)(2,1)} %get-tuple-element.24), channel_id=1, source_target_pairs={{0,26},{1,27},{2,28},{3,29},{4,30},{5,31},{6,0},{7,1},{8,2},{9,3},... | collective-permute-start | bytes 811016 | tf_op jit(solution)/shard_map/ppermute | solution.py:375
  26.4 1.2 %copy-start = (bf16[129,16,256]{2,1,0:T(8,128)(2,1)S(1)}, bf16[129,16,256]{2,1,0:T(8,128)(2,1)}, u32[]{:S(2)}) copy-start(bf16[129,16,256]{2,1,0:T(8,128)(2,1)} %get-tuple-element.19.refs_0_.refs_1_) | copy-start | bytes 3170308
  27.6 0.7 %copy-start.1 = (s32[1,4]{1,0:T(1,128)S(1)}, s32[1,4]{1,0:T(1,128)}, u32[]{:S(2)}) copy-start(s32[1,4]{1,0:T(1,128)} %refs_0_.3) | copy-start | bytes 52
  28.2 4.1 %copy-start.3 = (bf16[33,16,256]{2,1,0:T(8,128)(2,1)S(1)}, bf16[33,16,256]{2,1,0:T(8,128)(2,1)}, u32[]{:S(2)}) copy-start(bf16[33,16,256]{2,1,0:T(8,128)(2,1)} %get-tuple-element.27) | copy-start | bytes 811012
  28.2 6.6 %copy-start.2 = (bf16[33,16,256]{2,1,0:T(8,128)(2,1)S(1)}, bf16[33,16,256]{2,1,0:T(8,128)(2,1)}, u32[]{:S(2)}) copy-start(bf16[33,16,256]{2,1,0:T(8,128)(2,1)} %get-tuple-element.23) | copy-start | bytes 811012
  32.3 14.5 %collective-permute-start.5 = (bf16[33,16,256]{2,1,0:T(8,128)(2,1)S(1)}, bf16[33,16,256]{2,1,0:T(8,128)(2,1)S(1)}, u32[]{:S(2)}, u32[]{:S(2)}) collective-permute-start(bf16[33,16,256]{2,1,0:T(8,128)(2,1)S(1)} %copy-done.3), channel_id=1, source_target_pairs={{0,27},{1,26},{2,29},{3,28},{4,31},{5,30},{6,1},{7,0},{8,3},{9,2},... | collective-permute-start | bytes 811016 | tf_op jit(solution)/shard_map/ppermute | solution.py:375
  34.9 14.5 %collective-permute-start.3 = (bf16[33,16,256]{2,1,0:T(8,128)(2,1)S(1)}, bf16[33,16,256]{2,1,0:T(8,128)(2,1)S(1)}, u32[]{:S(2)}, u32[]{:S(2)}) collective-permute-start(bf16[33,16,256]{2,1,0:T(8,128)(2,1)S(1)} %copy-done.2), channel_id=1, source_target_pairs={{0,29},{1,28},{2,31},{3,30},{4,1},{5,0},{6,3},{7,2},{8,5},{9,4},{1... | collective-permute-start | bytes 811016 | tf_op jit(solution)/shard_map/ppermute | solution.py:375

commit v5 on v4

--- a/solution.py
+++ b/solution.py
@@ -250,9 +250,12 @@
         for slots, copies in ((depth, out_copies), (1, zero_copies)):
             copies.append(
                 [
-                    pltpu.make_async_copy(
-                        ring.at[i, c % slots, :, pl.ds(0, size)], out.at[0, pair, :, pl.ds(first, size)], out_sem.at[i, c]
-                    )
+                    [
+                        pltpu.make_async_copy(
+                            ring.at[i, c % slots, r, pl.ds(0, size)], out.at[0, pair, r, pl.ds(first, size)], out_sem.at[i, c, r]
+                        )
+                        for r in range(2)
+                    ]
                     for c, (first, size) in enumerate(chunks[i])
                 ]
             )
@@ -275,9 +278,9 @@
         @pl.when(live == 0)
         def _(i=i):
             ring[i, 0] = jnp.zeros(ring.shape[2:], ring.dtype)
-            for c, copy in enumerate(zero_copies[i]):
+            for copy in sum(zero_copies[i], []):
                 copy.start()
-            for copy in zero_copies[i][:-depth]:
+            for copy in sum(zero_copies[i][:-depth], []):
                 copy.wait()
 
         @pl.when(live != 0)
@@ -286,7 +289,8 @@
             weight[...] = by_row * inv_rms_of([held[k, 0] for k in y_power], samples)
             for c, (first, size) in enumerate(chunks[i]):
                 if c >= depth:
-                    out_copies[i][c - depth].wait()
+                    for copy in out_copies[i][c - depth]:
+                        copy.wait()
                 for f in range(first, first + size):
                     x = jnp.concatenate([held[k, f] for k in x_loads], axis=0)
                     y = jnp.concatenate([held[k, f] for k in y_loads], axis=0)
@@ -296,10 +300,11 @@
                     for r in range(2):
                         part = product[:, r * width : (r + 1) * width] * weight[...]
                         ring[i, c % depth, r, f - first] = part.astype(ring.dtype)
-                out_copies[i][c].start()
+                for copy in out_copies[i][c]:
+                    copy.start()
 
     for copies in out_copies:
-        for copy in copies[-depth:]:
+        for copy in sum(copies[-depth:], []):
             copy.wait()
 
 
@@ -339,7 +344,7 @@
             pltpu.VMEM((width, width), jnp.float32),
             pltpu.SemaphoreType.DMA,
             pltpu.SemaphoreType.DMA((len(slots),)),
-            pltpu.SemaphoreType.DMA((len(pairs), bins // min(CHUNK, bins) + 2)),
+            pltpu.SemaphoreType.DMA((len(pairs), bins // min(CHUNK, bins) + 2, 2)),
         ],
         out_shape=jax.ShapeDtypeStruct(shape, jnp.bfloat16),
         input_output_aliases=aliases,

time: 58 us -> 58.5 us (level)
  starting transfers between devices: 17.4 us -> 15.9 us
  Pallas kernels: 30.9 us -> 32.2 us
  waiting for transfers between devices: 6.98 us -> 7.67 us
    ppermute x8, starting transfers between devices: 17.4 us -> 15.9 us  [delivered(): return lax.ppermute(cut, ('chan', 'seg'), route)]
    pallas_call x3, Pallas kernels: 16.7 us -> 18.1 us  [cross(): pl.pallas_call(kernel, in_specs=[in_hbm if a is sched or a is kept else a...]
    ppermute x8, waiting for transfers between devices: 6.98 us -> 7.67 us  [delivered(): return lax.ppermute(cut, ('chan', 'seg'), route)]
  transfers between devices with their start and end apart: 8 -> 8, of which waited for: 3 -> 3; matrix products, arithmetic and copies ran while one was open for 0% -> 0% of each run, Pallas kernels for 30% -> 31%
where the time goes in v5:
time: 58.5 us; the launch traced here: 57.9 us
  Pallas kernels  32.2 us (55%)
  starting transfers between devices  15.9 us (27%)
  waiting for transfers between devices  7.67 us (13%)
  local copies, waits for them, and re-layouts  1.89 us (3%)
    pallas_call x3, Pallas kernels, cross(): pl.pallas_call(kernel, in_specs=[in_hbm if a is sched or a is kept else a...  18.1 us
    ppermute x8, starting transfers between devices, delivered(): return lax.ppermute(cut, ('chan', 'seg'), route)  15.9 us
    pallas_call x1, Pallas kernels, make_spectra(): pl.pallas_call(functools.partial(spectra_kernel, plan, seg), in_specs=[pl...  8.42 us
    ppermute x8, waiting for transfers between devices, delivered(): return lax.ppermute(cut, ('chan', 'seg'), route)  7.67 us
    pallas_call x1, Pallas kernels, early_spectra(): pl.pallas_call(functools.partial(early_kernel, plan, seg), in_specs=[pl.B...  5.72 us
    unnamed x8, local copies, waits for them, and re-layouts  1.89 us
  transfers between devices with their start and end apart: 8, of which 3 were waited for; matrix products, arithmetic and copies ran while one was open for 0% of the time, Pallas kernels for 31%

profile of v5, /device:TPU:0, one launch (start us, length us, event | category | flops | bytes accessed | tf_op | source)
XLA Modules:
  0.0 57.9 jit_solution(436405590012546290)
XLA Ops:
  0.0 5.7 %shard_map.55 = (bf16[65,16,256]{2,1,0:T(8,128)(2,1)}, bf16[33,16,256]{2,1,0:T(8,128)(2,1)}) custom-call(s32[4,16]{1,0:T(4,128)} %bitcast.1, f32[2,8,264,128]{3,2,1,0:T(8,128)} %constant.4.clone.rows_hbm, bf16[8,1024,256]{2,1,0:T(8,128)(2,1)} %signal_hbm.3), custom_call_target="tpu_custom_call" | custom-call | tf_op jit(solution)/shard_map/pallas_call | solution.py:132
  5.7 3.0 %collective-permute-start.2 = (bf16[65,16,256]{2,1,0:T(8,128)(2,1)}, bf16[65,16,256]{2,1,0:T(8,128)(2,1)S(1)}, u32[]{:S(2)}, u32[]{:S(2)}) collective-permute-start(bf16[65,16,256]{2,1,0:T(8,128)(2,1)} %get-tuple-element.18.early_hbm), channel_id=1, source_target_pairs={{0,1},{1,0},{2,3},{3,2},{4,5},{5,4},{6,7},{7,6},{8,9},{9,8},{10,11... | collective-permute-start | bytes 1597448 | tf_op jit(solution)/shard_map/ppermute | solution.py:380
  8.7 3.7 %collective-permute-start.7 = (bf16[33,16,256]{2,1,0:T(8,128)(2,1)}, bf16[33,16,256]{2,1,0:T(8,128)(2,1)S(1)}, u32[]{:S(2)}, u32[]{:S(2)}) collective-permute-start(bf16[33,16,256]{2,1,0:T(8,128)(2,1)} %get-tuple-element.29), channel_id=1, source_target_pairs={{0,31},{1,30},{2,1},{3,0},{4,3},{5,2},{6,5},{7,4},{8,7},{9,6},{10,... | collective-permute-start | bytes 811016 | tf_op jit(solution)/shard_map/ppermute | solution.py:380
  12.4 8.4 %shard_map.56 = (bf16[33,16,256]{2,1,0:T(8,128)(2,1)}, bf16[33,16,256]{2,1,0:T(8,128)(2,1)}, bf16[33,16,256]{2,1,0:T(8,128)(2,1)}, bf16[64,16,256]{2,1,0:T(8,128...) custom-call(s32[4,16]{1,0:T(4,128)} %bitcast.2, ...), custom_call_target="tpu_custom_call" | custom-call | flops 2147483648 | bytes 33554432 | tf_op jit(solution)/shard_map/pallas_call | solution.py:195
  20.8 1.2 %collective-permute-start.6 = (bf16[33,16,256]{2,1,0:T(8,128)(2,1)}, bf16[33,16,256]{2,1,0:T(8,128)(2,1)S(1)}, u32[]{:S(2)}, u32[]{:S(2)}) collective-permute-start(bf16[33,16,256]{2,1,0:T(8,128)(2,1)} %get-tuple-element.28), channel_id=1, source_target_pairs={{0,30},{1,31},{2,0},{3,1},{4,2},{5,3},{6,4},{7,5},{8,6},{9,7},{10,... | collective-permute-start | bytes 811016 | tf_op jit(solution)/shard_map/ppermute | solution.py:380
  22.0 1.5 %collective-permute-start = (bf16[64,16,256]{2,1,0:T(8,128)(2,1)}, bf16[64,16,256]{2,1,0:T(8,128)(2,1)S(1)}, u32[]{:S(2)}, u32[]{:S(2)}) collective-permute-start(bf16[64,16,256]{2,1,0:T(8,128)(2,1)} %get-tuple-element.20), channel_id=1, source_target_pairs={{0,1},{1,0},{2,3},{3,2},{4,5},{5,4},{6,7},{7,6},{8,9},{9,8},{10,11... | collective-permute-start | bytes 1572872 | tf_op jit(solution)/shard_map/ppermute | solution.py:380
  23.5 0.5 collective-permute-start.1
  24.0 0.7 %collective-permute-done.2.refs_1_.refs_2_.refs_5_ = bf16[65,16,256]{2,1,0:T(8,128)(2,1)S(1)} collective-permute-done((bf16[65,16,256]{2,1,0:T(8,128)(2,1)}, bf16[65,16,256]{2,1,0:T(8,128)(2,1)S(1)}, u32[]{:S(2)}, u32[]{:S(2)}) %collective-permute-start.2) | collective-permute-done | bytes 532512 | tf_op jit(solution)/shard_map/ppermute | solution.py:380
  24.8 1.6 %collective-permute-start.4 = (bf16[33,16,256]{2,1,0:T(8,128)(2,1)}, bf16[33,16,256]{2,1,0:T(8,128)(2,1)S(1)}, u32[]{:S(2)}, u32[]{:S(2)}) collective-permute-start(bf16[33,16,256]{2,1,0:T(8,128)(2,1)} %get-tuple-element.24), channel_id=1, source_target_pairs={{0,26},{1,27},{2,28},{3,29},{4,30},{5,31},{6,0},{7,1},{8,2},{9,3},... | collective-permute-start | bytes 811016 | tf_op jit(solution)/shard_map/ppermute | solution.py:380
  26.4 0.0 copy-start
  26.4 1.2 %copy-done = bf16[129,16,256]{2,1,0:T(8,128)(2,1)S(1)} copy-done((bf16[129,16,256]{2,1,0:T(8,128)(2,1)S(1)}, bf16[129,16,256]{2,1,0:T(8,128)(2,1)}, u32[]{:S(2)}) %copy-start) | copy-done | bytes 1056792
  27.6 0.0 copy-start.1
  27.6 0.7 %copy-done.1 = s32[1,4]{1,0:T(1,128)S(1)} copy-done((s32[1,4]{1,0:T(1,128)S(1)}, s32[1,4]{1,0:T(1,128)}, u32[]{:S(2)}) %copy-start.1) | copy-done | bytes 40
  28.2 0.0 copy-start.3
  28.2 0.0 copy-start.2
  28.2 4.8 %shard_map.57.refs_5_ = bf16[1,4,2,32,256,256]{5,4,3,2,1,0:T(8,128)(2,1)} custom-call(s32[1,4]{1,0:T(1,128)S(1)} %copy-done.1, bf16[129,16,256]{2,1,0:T(8,128)(2,1)S(1)} %copy-done, bf16[65,16,256]{2,1,0:T(8,128)(2,1)S(1)} %collective-permute-done.2.refs_1_.refs_2_.refs_5_), custom_call_target="tpu_custom_call" | custom-call | flops 268435456 | bytes 8388608 | tf_op jit(solution)/shard_map/pallas_call | solution.py:336
  33.1 0.0 collective-permute-done.7.refs_4_
  33.1 0.0 copy-done.3
  33.1 1.8 %collective-permute-start.5 = (bf16[33,16,256]{2,1,0:T(8,128)(2,1)S(1)}, bf16[33,16,256]{2,1,0:T(8,128)(2,1)S(1)}, u32[]{:S(2)}, u32[]{:S(2)}) collective-permute-start(bf16[33,16,256]{2,1,0:T(8,128)(2,1)S(1)} %copy-done.3), channel_id=1, source_target_pairs={{0,27},{1,26},{2,29},{3,28},{4,31},{5,30},{6,1},{7,0},{8,3},{9,2},... | collective-permute-start | bytes 811016 | tf_op jit(solution)/shard_map/ppermute | solution.py:380
  34.9 0.0 collective-permute-done.6.refs_3_
  34.9 0.0 copy-done.2
  34.9 2.6 %collective-permute-start.3 = (bf16[33,16,256]{2,1,0:T(8,128)(2,1)S(1)}, bf16[33,16,256]{2,1,0:T(8,128)(2,1)S(1)}, u32[]{:S(2)}, u32[]{:S(2)}) collective-permute-start(bf16[33,16,256]{2,1,0:T(8,128)(2,1)S(1)} %copy-done.2), channel_id=1, source_target_pairs={{0,29},{1,28},{2,31},{3,30},{4,1},{5,0},{6,3},{7,2},{8,5},{9,4},{1... | collective-permute-start | bytes 811016 | tf_op jit(solution)/shard_map/ppermute | solution.py:380
  37.5 4.9 %shard_map.58.refs_8_ = bf16[1,4,2,32,256,256]{5,4,3,2,1,0:T(8,128)(2,1)} custom-call(s32[1,4]{1,0:T(1,128)S(1)} %copy-done.1, bf16[129,16,256]{2,1,0:T(8,128)(2,1)S(1)} %copy-done, bf16[65,16,256]{2,1,0:T(8,128)(2,1)S(1)} %collective-permute-done.2.refs_1_.refs_2_.refs_5_, ...), custom_call_target="tpu_custom_call", output_to_operand_aliasing={{}: (5, {})} | custom-call | flops 268435456 | bytes 8388608 | tf_op jit(solution)/shard_map/pallas_call | solution.py:336
  42.4 0.0 collective-permute-done.1.refs_3_
  42.4 0.0 collective-permute-done.4.refs_6_
  42.5 0.0 collective-permute-done.refs_2_
  42.5 4.3 %collective-permute-done.5.refs_7_ = bf16[33,16,256]{2,1,0:T(8,128)(2,1)S(1)} collective-permute-done((bf16[33,16,256]{2,1,0:T(8,128)(2,1)S(1)}, bf16[33,16,256]{2,1,0:T(8,128)(2,1)S(1)}, u32[]{:S(2)}, u32[]{:S(2)}) %collective-permute-start.5) | collective-permute-done | bytes 270368 | tf_op jit(solution)/shard_map/ppermute | solution.py:380
  46.8 2.6 %collective-permute-done.3.refs_4_ = bf16[33,16,256]{2,1,0:T(8,128)(2,1)S(1)} collective-permute-done((bf16[33,16,256]{2,1,0:T(8,128)(2,1)S(1)}, bf16[33,16,256]{2,1,0:T(8,128)(2,1)S(1)}, u32[]{:S(2)}, u32[]{:S(2)}) %collective-permute-start.3) | collective-permute-done | bytes 270368 | tf_op jit(solution)/shard_map/ppermute | solution.py:380
  49.4 8.4 %shard_map.59 = bf16[1,4,2,32,256,256]{5,4,3,2,1,0:T(8,128)(2,1)} custom-call(s32[1,4]{1,0:T(1,128)S(1)} %copy-done.1, bf16[129,16,256]{2,1,0:T(8,128)(2,1)S(1)} %copy-done, bf16[64,16,256]{2,1,0:T(8,128)(2,1)S(1)} %collective-permute-done.refs_2_, bf16[33,16,256]{2,1,0:T(8,128)(2,1)S(1)} %collective-permute-done.1.refs_3_, ...), custom_call_target="tpu_custom_call", output_to_operand_aliasing={{}: (8, {})} | custom-call | flops 536870912 | bytes 16777216 | tf_op jit(solution)/shard_map/pallas_call | solution.py:336
Async XLA Ops:
  5.7 19.0 %collective-permute-start.2 = (bf16[65,16,256]{2,1,0:T(8,128)(2,1)}, bf16[65,16,256]{2,1,0:T(8,128)(2,1)S(1)}, u32[]{:S(2)}, u32[]{:S(2)}) collective-permute-start(bf16[65,16,256]{2,1,0:T(8,128)(2,1)} %get-tuple-element.18.early_hbm), channel_id=1, source_target_pairs={{0,1},{1,0},{2,3},{3,2},{4,5},{5,4},{6,7},{7,6},{8,9},{9,8},{10,11... | collective-permute-start | bytes 1597448 | tf_op jit(solution)/shard_map/ppermute | solution.py:380
  8.7 24.4 %collective-permute-start.7 = (bf16[33,16,256]{2,1,0:T(8,128)(2,1)}, bf16[33,16,256]{2,1,0:T(8,128)(2,1)S(1)}, u32[]{:S(2)}, u32[]{:S(2)}) collective-permute-start(bf16[33,16,256]{2,1,0:T(8,128)(2,1)} %get-tuple-element.29), channel_id=1, source_target_pairs={{0,31},{1,30},{2,1},{3,0},{4,3},{5,2},{6,5},{7,4},{8,7},{9,6},{10,... | collective-permute-start | bytes 811016 | tf_op jit(solution)/shard_map/ppermute | solution.py:380
  20.8 14.1 %collective-permute-start.6 = (bf16[33,16,256]{2,1,0:T(8,128)(2,1)}, bf16[33,16,256]{2,1,0:T(8,128)(2,1)S(1)}, u32[]{:S(2)}, u32[]{:S(2)}) collective-permute-start(bf16[33,16,256]{2,1,0:T(8,128)(2,1)} %get-tuple-element.28), channel_id=1, source_target_pairs={{0,30},{1,31},{2,0},{3,1},{4,2},{5,3},{6,4},{7,5},{8,6},{9,7},{10,... | collective-permute-start | bytes 811016 | tf_op jit(solution)/shard_map/ppermute | solution.py:380
  22.0 20.4 %collective-permute-start = (bf16[64,16,256]{2,1,0:T(8,128)(2,1)}, bf16[64,16,256]{2,1,0:T(8,128)(2,1)S(1)}, u32[]{:S(2)}, u32[]{:S(2)}) collective-permute-start(bf16[64,16,256]{2,1,0:T(8,128)(2,1)} %get-tuple-element.20), channel_id=1, source_target_pairs={{0,1},{1,0},{2,3},{3,2},{4,5},{5,4},{6,7},{7,6},{8,9},{9,8},{10,11... | collective-permute-start | bytes 1572872 | tf_op jit(solution)/shard_map/ppermute | solution.py:380
  23.5 18.9 %collective-permute-start.1 = (bf16[33,16,256]{2,1,0:T(8,128)(2,1)}, bf16[33,16,256]{2,1,0:T(8,128)(2,1)S(1)}, u32[]{:S(2)}, u32[]{:S(2)}) collective-permute-start(bf16[33,16,256]{2,1,0:T(8,128)(2,1)} %get-tuple-element.21), channel_id=1, source_target_pairs={{0,28},{1,29},{2,30},{3,31},{4,0},{5,1},{6,2},{7,3},{8,4},{9,5},{1... | collective-permute-start | bytes 811016 | tf_op jit(solution)/shard_map/ppermute | solution.py:380
  24.8 17.7 %collective-permute-start.4 = (bf16[33,16,256]{2,1,0:T(8,128)(2,1)}, bf16[33,16,256]{2,1,0:T(8,128)(2,1)S(1)}, u32[]{:S(2)}, u32[]{:S(2)}) collective-permute-start(bf16[33,16,256]{2,1,0:T(8,128)(2,1)} %get-tuple-element.24), channel_id=1, source_target_pairs={{0,26},{1,27},{2,28},{3,29},{4,30},{5,31},{6,0},{7,1},{8,2},{9,3},... | collective-permute-start | bytes 811016 | tf_op jit(solution)/shard_map/ppermute | solution.py:380
  26.4 1.2 %copy-start = (bf16[129,16,256]{2,1,0:T(8,128)(2,1)S(1)}, bf16[129,16,256]{2,1,0:T(8,128)(2,1)}, u32[]{:S(2)}) copy-start(bf16[129,16,256]{2,1,0:T(8,128)(2,1)} %get-tuple-element.19.refs_0_.refs_1_) | copy-start | bytes 3170308
  27.6 0.7 %copy-start.1 = (s32[1,4]{1,0:T(1,128)S(1)}, s32[1,4]{1,0:T(1,128)}, u32[]{:S(2)}) copy-start(s32[1,4]{1,0:T(1,128)} %refs_0_.3) | copy-start | bytes 52
  28.2 4.9 %copy-start.3 = (bf16[33,16,256]{2,1,0:T(8,128)(2,1)S(1)}, bf16[33,16,256]{2,1,0:T(8,128)(2,1)}, u32[]{:S(2)}) copy-start(bf16[33,16,256]{2,1,0:T(8,128)(2,1)} %get-tuple-element.27) | copy-start | bytes 811012
  28.2 6.7 %copy-start.2 = (bf16[33,16,256]{2,1,0:T(8,128)(2,1)S(1)}, bf16[33,16,256]{2,1,0:T(8,128)(2,1)}, u32[]{:S(2)}) copy-start(bf16[33,16,256]{2,1,0:T(8,128)(2,1)} %get-tuple-element.23) | copy-start | bytes 811012
  33.1 13.7 %collective-permute-start.5 = (bf16[33,16,256]{2,1,0:T(8,128)(2,1)S(1)}, bf16[33,16,256]{2,1,0:T(8,128)(2,1)S(1)}, u32[]{:S(2)}, u32[]{:S(2)}) collective-permute-start(bf16[33,16,256]{2,1,0:T(8,128)(2,1)S(1)} %copy-done.3), channel_id=1, source_target_pairs={{0,27},{1,26},{2,29},{3,28},{4,31},{5,30},{6,1},{7,0},{8,3},{9,2},... | collective-permute-start | bytes 811016 | tf_op jit(solution)/shard_map/ppermute | solution.py:380
  34.9 14.5 %collective-permute-start.3 = (bf16[33,16,256]{2,1,0:T(8,128)(2,1)S(1)}, bf16[33,16,256]{2,1,0:T(8,128)(2,1)S(1)}, u32[]{:S(2)}, u32[]{:S(2)}) collective-permute-start(bf16[33,16,256]{2,1,0:T(8,128)(2,1)S(1)} %copy-done.2), channel_id=1, source_target_pairs={{0,29},{1,28},{2,31},{3,30},{4,1},{5,0},{6,3},{7,2},{8,5},{9,4},{1... | collective-permute-start | bytes 811016 | tf_op jit(solution)/shard_map/ppermute | solution.py:380
